TPU v7x, 128 devices: a whole 4x4x4 slice. The times are simulated.
128 devices in a mesh: head: 8 (over x_lo, z), wide: 16 (over x_hi, y, core).
Axes of the slice: x: 4 (x_hi: 2, x_lo: 2; x = x_hi * 2 + x_lo), y: 4, z: 4, core: 2. Of those that a mesh axis runs over, the one named last changes fastest.
Arguments:
- queries: bfloat16 [1024, 8192], P('wide', 'head'), may hold values from -16 to 16
- fresh_keys: bfloat16 [1024, 1024], P('wide', 'head'), may hold values from -16 to 16
- fresh_values: bfloat16 [1024, 1024], P('wide', 'head'), may hold values from -5 to 5
- cached_keys: bfloat16 [16, 2048, 1024], P('wide', None, 'head'), may hold values from -10 to 10
- cached_values: bfloat16 [16, 2048, 1024], P('wide', None, 'head'), may hold values from -5 to 5
- context_len: int32 [16], P('wide'), may hold values from 512 to 2048, as said below
- tree_size: int32 [16], P('wide'), may hold values from 16 to 64, as said below
- parents: int32 [16, 64], P('wide'), may hold values from 0 to 62, as said below
- residual: bfloat16 [1024, 8192], P(None, 'wide'), may hold values from -36 to 36
- out_weight: bfloat16 [8192, 8192], P('head', 'wide'), may hold values from -0.0625 to 0.0625
- gate_up_weight: bfloat16 [8192, 2, 28672], P('wide', None, 'head'), may hold values from -0.0625 to 0.0625
- down_weight: bfloat16 [28672, 8192], P('head', 'wide'), may hold values from -0.03125 to 0.03125
Outputs:
- attended: bfloat16 [1024, 8192], P('head', 'wide')
- update: bfloat16 [1024, 8192], P('head', 'wide')
Inputs may be any that keep to these rules, and one draw needn't show every extreme that they name: `context_len`: some request has exactly 2048. `tree_size`: a multiple of 16; some request has exactly 64. `parents`: node 0 is each tree's root and its own parent; every other node's parent is an earlier node.
All inputs are finite; a program needn't handle non-finite values.
Results may differ from a plain program's by a relative error of at most 0.035.
Values may be sent and summed in bfloat16 or wider, within the bound.
A program may use at most 128 MiB of HBM per device.

v0:
```python
import math

import jax
import jax.numpy as jnp
from jax import lax
from jax.sharding import PartitionSpec as P

D = 8192
HEADS = 64
KV = 8
HD = 128


epsilon = 1e-05


def ancestry(parent_row, node_count):
    node_ids = jnp.arange(node_count, dtype=jnp.int32)
    linked = (parent_row[:, None] == node_ids[None, :]) | (node_ids[:, None] == node_ids[None, :])
    reached = linked.astype(jnp.float32)
    for squaring in range(max(1, (node_count - 1).bit_length())):
        reached = jnp.minimum(jnp.dot(reached, reached, precision=lax.Precision.HIGHEST), 1.0)
    return reached > 0.5


def attend_request(
    query_block, cache_keys, cache_values, tree_keys, tree_values, length, live_count, parent_row
):
    node_count = query_block.shape[0]
    score_scale = 1.0 / math.sqrt(query_block.shape[-1])
    visible = ancestry(parent_row, node_count)
    positions = jnp.arange(cache_keys.shape[0], dtype=jnp.int32)
    node_ids = jnp.arange(node_count, dtype=jnp.int32)
    cache_open = positions < length
    tree_open = visible & (node_ids[None, :] < live_count)
    cache_scores = (
        jnp.einsum("tkgd,ckd->kgtc", query_block, cache_keys, preferred_element_type=jnp.float32)
        * score_scale
    )
    tree_scores = (
        jnp.einsum("tkgd,ukd->kgtu", query_block, tree_keys, preferred_element_type=jnp.float32)
        * score_scale
    )
    cache_scores = jnp.where(cache_open[None, None, None, :], cache_scores, -1e30)
    tree_scores = jnp.where(tree_open[None, None], tree_scores, -1e30)
    row_max = jnp.maximum(jnp.max(cache_scores, axis=-1), jnp.max(tree_scores, axis=-1))
    cache_probs = jnp.exp(cache_scores - row_max[..., None])
    tree_probs = jnp.exp(tree_scores - row_max[..., None])
    denominator = jnp.sum(cache_probs, axis=-1) + jnp.sum(tree_probs, axis=-1)
    gathered = jnp.einsum(
        "kgtc,ckd->tkgd",
        cache_probs.astype(jnp.bfloat16),
        cache_values,
        preferred_element_type=jnp.float32,
    )
    gathered = gathered + jnp.einsum(
        "kgtu,ukd->tkgd",
        tree_probs.astype(jnp.bfloat16),
        tree_values,
        preferred_element_type=jnp.float32,
    )
    result = gathered / jnp.transpose(denominator, (2, 0, 1))[..., None]
    live_rows = node_ids < live_count
    return jnp.where(live_rows[:, None, None, None], result, 0.0)


def per_device(
    queries,
    fresh_keys,
    fresh_values,
    cached_keys,
    cached_values,
    context_len,
    tree_size,
    parents,
    residual,
    out_weight,
    gate_up_weight,
    down_weight,
):
    node_count = queries.shape[0]
    kv_local = fresh_keys.shape[1] // HD
    groups = HEADS // KV
    query_heads = queries.reshape(node_count, kv_local, groups, HD)
    cache_k = cached_keys.reshape(-1, kv_local, HD)
    cache_v = cached_values.reshape(-1, kv_local, HD)
    tree_k = fresh_keys.reshape(node_count, kv_local, HD)
    tree_v = fresh_values.reshape(node_count, kv_local, HD)
    attention = attend_request(
        query_heads, cache_k, cache_v, tree_k, tree_v, context_len[0], tree_size[0], parents[0]
    )
    attention_rows = attention.reshape(node_count, kv_local * groups * HD).astype(jnp.bfloat16)
    partial_value = jnp.dot(
        lax.all_gather(attention_rows, "wide", axis=0, tiled=True),
        out_weight,
        preferred_element_type=jnp.float32,
    )
    projection = lax.psum(partial_value.astype(jnp.bfloat16), "head").astype(jnp.float32)
    combined = residual.astype(jnp.float32) + projection
    total_rows = combined.shape[0]
    row_share = total_rows // lax.axis_size("head")
    attended = lax.dynamic_slice_in_dim(
        combined, lax.axis_index("head") * row_share, row_share, 0
    ).astype(jnp.bfloat16)
    squares = lax.psum(jnp.sum(combined * combined, axis=1), "wide")
    normed = (combined * lax.rsqrt(squares[:, None] / D + epsilon)).astype(jnp.bfloat16)
    width_local = gate_up_weight.shape[2]
    stacked = gate_up_weight.reshape(gate_up_weight.shape[0], 2 * width_local)
    summed = lax.psum_scatter(
        jnp.dot(normed, stacked, preferred_element_type=jnp.float32).astype(jnp.bfloat16),
        "wide",
        scatter_dimension=0,
        tiled=True,
    ).astype(jnp.float32)
    hidden = (jax.nn.silu(summed[:, :width_local]) * summed[:, width_local:]).astype(jnp.bfloat16)
    down_part = jnp.dot(
        lax.all_gather(hidden, "wide", axis=0, tiled=True),
        down_weight,
        preferred_element_type=jnp.float32,
    )
    update = lax.psum_scatter(
        down_part.astype(jnp.bfloat16), "head", scatter_dimension=0, tiled=True
    )
    return (attended, update)


def solution(mesh):
    placed = (
        P("wide", "head"),
        P("wide", "head"),
        P("wide", "head"),
        P("wide", None, "head"),
        P("wide", None, "head"),
        P("wide"),
        P("wide"),
        P("wide", None),
        P(None, "wide"),
        P("head", "wide"),
        P("wide", None, "head"),
        P("head", "wide"),
    )
    return jax.shard_map(
        per_device,
        mesh=mesh,
        in_specs=placed,
        out_specs=(P("head", "wide"), P("head", "wide")),
        check_vma=False,
    )
```

profile of v0, /device:TPU:8, one launch (start us, length us, event | category | flops | bytes accessed | tf_op | source)
XLA Modules:
  0.0 445.6 jit_solution(1982076397138937660)
XLA Ops:
  8.6 0.9 convolution_minimum_fusion.5
  9.6 0.2 convolution_minimum_fusion.4
  9.8 0.2 convolution_minimum_fusion.3
  9.9 0.2 convolution_minimum_fusion.2
  10.1 0.2 convolution_minimum_fusion.1
  10.3 0.2 fusion.11
  10.4 0.1 copy.19
  10.5 1.9 bitcast_reduce_fusion
  12.5 0.3 fusion.36
  12.8 1.0 fusion.1
  13.7 0.1 fusion.20
  13.8 1.0 fusion.4
  14.8 0.2 fusion.14
  15.1 0.1 copy.22
  15.2 0.7 copy.40
  15.9 0.0 all-reduce.2.cloned.1.call-start
  15.9 49.5 %all-gather.3.cloned.1.call-done = bf16[1024,1024]{1,0:T(8,128)(2,1)} async-done(((bf16[64,1024]{1,0:T(8,128)(2,1)}), bf16[1024,1024]{1,0:T(8,128)(2,1)}) %all-gather.3.cloned.1.call-update) | async-done | bytes 2097168 | tf_op jit(solution)/shard_map/all_gather | solution.py:94
  65.5 3.8 convolution_convert_fusion.2
  69.4 7.9 %copy.26 = bf16[64,8,2,3584]{3,1,2,0:T(8,128)(2,1)} copy(bf16[64,8,2,3584]{3,2,1,0:T(2,128)(2,1)} %bitcast.117) | data formatting | bytes 14680064
  77.2 68.7 %all-reduce.2.cloned.1.call-done = bf16[1024,512]{1,0:T(8,128)(2,1)} async-done(((bf16[1024,512]{1,0:T(8,128)(2,1)}), bf16[1024,512]{1,0:T(8,128)(2,1)}) %all-reduce.2.cloned.1.call-update) | async-done | bytes 1048592 | tf_op jit(solution)/shard_map/psum | solution.py:98
  145.9 1.6 multiply_reduce_fusion
  147.5 27.8 %psum.15 = f32[1024]{0:T(1024)S(1)} all-reduce(f32[1024]{0:T(1024)S(1)} %multiply_reduce_fusion), channel_id=1, replica_groups=mesh['head'=8,'wide'=16] {'wide'}, use_global_device_ids=true, to_apply=%region_6.7 | all-reduce | flops 1024 | bytes 8192 | tf_op jit(solution)/shard_map/psum | solution.py:105
  175.4 13.5 %convolution_convert_fusion = bf16[1024,7168]{1,0:T(8,128)(2,1)} fusion(bf16[512,7168]{1,0:T(8,128)(2,1)} %bitcast.118, f32[1024]{0:T(1024)S(1)} %add_rsqrt_fusion, bf16[1024,512]{1,0:T(8,128)(2,1)} %all-reduce.2.cloned.1.call-done, bf16[1024,512]{1,0:T(8,128)(2,1)S(1)} %copy-done.1), kind=kOutput, calls=%fused_computation | convolution fusion | flops 7526154240 | bytes 24121344 | tf_op jit(solution)/shard_map/dot_general | solution.py:110
  188.9 0.0 all-gather.5.cloned.1.call-start
  188.9 133.7 %reduce-scatter.3.cloned.1.call-done = bf16[64,7168]{1,0:T(8,128)(2,1)} async-done(((bf16[1024,7168]{1,0:T(8,128)(2,1)}), bf16[64,7168]{1,0:T(8,128)(2,1)}) %reduce-scatter.3.cloned.1.call-update) | async-done | bytes 917520 | tf_op jit(solution)/shard_map/reduce_scatter | solution.py:109
  322.6 1.3 convert_element_type.50
  323.9 1.0 fusion.16
  325.0 66.4 %all-gather.5.cloned.1.call-done = bf16[1024,3584]{1,0:T(8,128)(2,1)} async-done(((bf16[64,3584]{1,0:T(8,128)(2,1)}), bf16[1024,3584]{1,0:T(8,128)(2,1)}) %all-gather.5.cloned.1.call-update) | async-done | bytes 7340048 | tf_op jit(solution)/shard_map/all_gather | solution.py:117
  391.4 9.0 %convolution_convert_fusion.1 = bf16[1024,512]{1,0:T(8,128)(2,1)} fusion(bf16[1024,3584]{1,0:T(8,128)(2,1)} %all-gather.5.cloned.1.call-done, bf16[3584,512]{1,0:T(8,128)(2,1)} %param.23), kind=kOutput, calls=%fused_computation.13 | convolution fusion | flops 3758620672 | bytes 12058624 | tf_op jit(solution)/shard_map/dot_general | solution.py:116
  400.5 0.3 convert_add_fusion
  400.8 0.7 dynamic-slice_convert_fusion
  401.5 37.6 %reduce-scatter.5.cloned.1.call-done = bf16[128,512]{1,0:T(8,128)(2,1)} async-done(((bf16[1024,512]{1,0:T(8,128)(2,1)}), bf16[128,512]{1,0:T(8,128)(2,1)}) %reduce-scatter.5.cloned.1.call-update) | async-done | bytes 131088 | tf_op jit(solution)/shard_map/reduce_scatter | solution.py:121
  (27 shorter events, 0.3 us)
Async XLA Ops:
  7.2 58.3 %copy-start = (bf16[1024,512]{1,0:T(8,128)(2,1)S(1)}, bf16[1024,512]{1,0:T(8,128)(2,1)}, u32[]{:S(2)}) copy-start(bf16[1024,512]{1,0:T(8,128)(2,1)} %param.21) | copy-start | bytes 3145732
  7.2 5.3 %copy-start.3 = (bf16[64,1024]{1,0:T(8,128)(2,1)S(1)}, bf16[64,1024]{1,0:T(8,128)(2,1)}, u32[]{:S(2)}) copy-start(bf16[64,1024]{1,0:T(8,128)(2,1)} %param.12) | copy-start | bytes 393220
  7.2 5.3 %copy-start.4 = (bf16[64,128]{1,0:T(8,128)(2,1)S(1)}, bf16[64,128]{1,0:T(8,128)(2,1)}, u32[]{:S(2)}) copy-start(bf16[64,128]{1,0:T(8,128)(2,1)} %param.13) | copy-start | bytes 49156
  7.2 58.2 %all-gather.3.cloned.1.call-start = ((), (), s32[]{:S(2)}) async-start(), calls=%async_computation.2 | async-start | bytes 2228224 | tf_op jit(solution)/shard_map/all_gather | solution.py:94
  12.5 1.3 copy-start.5
  13.7 1.1 copy-start.6
  15.9 130.0 %all-reduce.2.cloned.1.call-start = ((), (), s32[]{:S(2)}) async-start(), calls=%async_computation.3 | async-start | bytes 2097152 | tf_op jit(solution)/shard_map/psum | solution.py:98
  69.3 253.3 %reduce-scatter.3.cloned.1.call-start = ((), (), s32[]{:S(2)}) async-start(), calls=%async_computation.4 | async-start | bytes 15597568 | tf_op jit(solution)/shard_map/reduce_scatter | solution.py:109
  69.3 76.6 %copy-start.1 = (bf16[1024,512]{1,0:T(8,128)(2,1)S(1)}, bf16[1024,512]{1,0:T(8,128)(2,1)}, u32[]{:S(2)}) copy-start(bf16[1024,512]{1,0:T(8,128)(2,1)} %param.20) | copy-start | bytes 3145732
  188.9 202.5 %all-gather.5.cloned.1.call-start = ((), (), s32[]{:S(2)}) async-start(), calls=%async_computation.5 | async-start | bytes 7798784 | tf_op jit(solution)/shard_map/all_gather | solution.py:117
  325.0 75.6 %copy-start.2 = (bf16[1024,512]{1,0:T(8,128)(2,1)S(1)}, bf16[1024,512]{1,0:T(8,128)(2,1)}, u32[]{:S(2)}) copy-start(bf16[1024,512]{1,0:T(8,128)(2,1)} %all-reduce.2.cloned.1.call-done) | copy-start | bytes 3145732
  325.0 114.1 %reduce-scatter.5.cloned.1.call-start = ((), (), s32[]{:S(2)}) async-start(), calls=%async_computation.6 | async-start | bytes 1179648 | tf_op jit(solution)/shard_map/reduce_scatter | solution.py:121
Sparse Core Ops, SparseCore 0:
  16.0 49.4 all-gather.2
  69.4 76.4 all-reduce.1
  189.0 133.5 reduce-scatter.2
  325.1 66.3 all-gather.4
  400.6 38.4 reduce-scatter.4
where the time goes:
time: 446 us
  waiting for transfers between devices  356 us (80%)
  matrix products  31.5 us (7%)
  blocking collectives  27.8 us (6%)
  between operations  15.4 us (3%)
  local copies, waits for them, and re-layouts  9.44 us (2%)
  other arithmetic  5.26 us (1%)
    reduce_scatter x1, waiting for transfers between devices, per_device(): lax.psum_scatter(jnp.dot(normed, stacked, preferred_element_type=jnp.floa...  134 us
    psum x1, waiting for transfers between devices, per_device(): lax.psum(partial_value.astype(jnp.bfloat16), 'head').astype(jnp.float32)  68.7 us
    all_gather x1, waiting for transfers between devices, per_device(): lax.all_gather(hidden, 'wide', axis=0, tiled=True)  66.4 us
    all_gather x1, waiting for transfers between devices, per_device(): lax.all_gather(attention_rows, 'wide', axis=0, tiled=True)  49.5 us
    reduce_scatter x1, waiting for transfers between devices, per_device(): lax.psum_scatter(down_part.astype(jnp.bfloat16), 'head', scatter_dimensio...  37.6 us
    psum x1, blocking collectives, per_device(): squares = lax.psum(jnp.sum(combined * combined, axis=1), 'wide')  27.8 us
    dot_general x1, matrix products, per_device(): jnp.dot(normed, stacked, preferred_element_type=jnp.float32)  13.5 us
    dot_general x1, matrix products, per_device(): jnp.dot(lax.all_gather(hidden, 'wide', axis=0, tiled=True), down_weight,...  9.04 us
  transfers between devices with their start and end apart: 5, of which 5 were waited for; matrix products, arithmetic and copies ran while one was open for 2% of the time, Pallas kernels for 0%

commit v1 on v0

--- a/solution.py
+++ b/solution.py
@@ -1,8 +1,11 @@
+import functools
 import math
 
 import jax
 import jax.numpy as jnp
 from jax import lax
+from jax.experimental import pallas as pl
+from jax.experimental.pallas import tpu as pltpu
 from jax.sharding import PartitionSpec as P
 
 D = 8192
@@ -10,8 +13,18 @@
 KV = 8
 HD = 128
 
-
 epsilon = 1e-05
+
+BF = jnp.bfloat16
+F32 = jnp.float32
+MESH = pl.DeviceIdType.MESH
+
+A_U = 512
+B_U = 384
+A_W = 2 * A_U
+B_W = 2 * B_U
+HALF = 2 * A_U + 2 * B_U
+H_OFF = (0, A_U, 2 * A_U, 2 * A_U + B_U)
 
 
 def ancestry(parent_row, node_count):
@@ -62,6 +75,410 @@
     result = gathered / jnp.transpose(denominator, (2, 0, 1))[..., None]
     live_rows = node_ids < live_count
     return jnp.where(live_rows[:, None, None, None], result, 0.0)
+
+
+def layer_kernel(
+    att, gw, dw, wo_hbm, res_hbm,
+    att_out, upd_out,
+    G, R0, R1, WC, DD, WO, RES, PP, RB, X, PA, PB, RA, RAX, RBX, RBY, SQ, SQR, H, PDO, PDS, PDI, FR,
+    lsem, ssem, rsem,
+):
+    h = lax.axis_index("head")
+    w = lax.axis_index("wide")
+    xh = w // 8
+    y = (w // 2) % 4
+    c = w % 2
+
+    def wide(dxh, dy):
+        return (((xh + dxh) % 2) * 4 + (y + dy + 4) % 4) * 2 + c
+
+    sib = (h, w + 1 - 2 * c)
+
+    def wdev(dxh, dy):
+        return (h, wide(dxh, dy))
+
+    def hdev(k):
+        return ((h + k) % 8, w)
+
+    names = {}
+    sent = []
+
+    def send(name, src, dst, dev):
+        i = names.setdefault(name, len(names))
+        cp = pltpu.make_async_remote_copy(
+            src_ref=src, dst_ref=dst, send_sem=ssem.at[i], recv_sem=rsem.at[i],
+            device_id=dev, device_id_type=MESH,
+        )
+        cp.start()
+        sent.append(cp)
+
+    def arrive(name, dst, dev):
+        i = names[name]
+        pltpu.make_async_remote_copy(
+            src_ref=dst, dst_ref=dst, send_sem=ssem.at[i], recv_sem=rsem.at[i],
+            device_id=dev, device_id_type=MESH,
+        ).wait_recv()
+
+    mine = pl.ds(pl.multiple_of(c * HALF, 128), HALF)
+    other = pl.ds(pl.multiple_of((1 - c) * HALF, 128), HALF)
+    loads = [
+        pltpu.make_async_copy(wo_hbm, WO, lsem.at[0]),
+        pltpu.make_async_copy(gw.at[:, :, mine], R0, lsem.at[1]),
+        pltpu.make_async_copy(dw.at[mine, :], DD.at[0], lsem.at[2]),
+        pltpu.make_async_copy(
+            res_hbm.at[pl.ds(pl.multiple_of(h * 128, 128), 128), :], RES, lsem.at[3]
+        ),
+    ]
+    for cp in loads:
+        cp.start()
+
+    partners = [sib]
+    partners += [wdev(dx, dy) for dx in range(2) for dy in range(4) if (dx, dy) != (0, 0)]
+    partners += [hdev(k) for k in range(1, 8)]
+    barrier = pltpu.get_barrier_semaphore()
+    for dev in partners:
+        pl.semaphore_signal(barrier, inc=1, device_id=dev, device_id_type=MESH)
+    pl.semaphore_wait(barrier, len(partners))
+
+    send("g_x", att, G.at[w], wdev(1, 0))
+    for dy in (1, 3, 2):
+        send(f"g_y{dy}", att, G.at[w], wdev(0, dy))
+    send("g_c", att, G.at[w], sib)
+    send("s_gw", gw.at[:, :, other], R1, sib)
+    send("s_dw", dw.at[other, :], DD.at[1], sib)
+    G[w] = att[...]
+
+    def untwist(raw, row0, lo, hi):
+        @pl.loop(lo, hi)
+        def _(i):
+            r = pl.ds(pl.multiple_of(i * 64, 64), 64)
+            o = pl.ds(pl.multiple_of(row0 + i * 64, 64), 64)
+            b = raw[r]
+            gate, up = b[:, 0, :], b[:, 1, :]
+            for p in range(4):
+                n = A_U if p < 2 else B_U
+                u = H_OFF[p]
+                WC[o, 2 * u : 2 * u + n] = gate[:, u : u + n]
+                WC[o, 2 * u + n : 2 * u + 2 * n] = up[:, u : u + n]
+
+    wxp = wide(1, 0)
+    arrive("g_x", G.at[wxp], wdev(1, 0))
+    for dy in (1, 3, 2):
+        send(f"g_xy{dy}", G.at[wxp], G.at[wxp], wdev(0, dy))
+    send("g_cx", G.at[wxp], G.at[wxp], sib)
+    for dx, tag in ((0, "y"), (1, "xy")):
+        for dy in (1, 3, 2):
+            src = wide(dx, -dy)
+            arrive(f"g_{tag}{dy}", G.at[src], wdev(0, -dy))
+            send(f"g_c{tag}{dy}", G.at[src], G.at[src], sib)
+    loads[1].wait()
+    untwist(R0, 0, 0, 2)
+    flip = 1 - 2 * c
+    arrive("g_c", G.at[w + flip], sib)
+    arrive("g_cx", G.at[wxp + flip], sib)
+    for dx, tag in ((0, "y"), (1, "xy")):
+        for dy in (1, 3, 2):
+            arrive(f"g_c{tag}{dy}", G.at[wide(dx, -dy) + flip], sib)
+
+    loads[0].wait()
+    for k in range(1, 9):
+        j = (h + k) % 8
+        rows = G[pl.ds(2 * j, 2)].reshape(128, 1024)
+        PP[j] = jnp.dot(rows, WO[...], preferred_element_type=F32).astype(BF)
+        if k < 8:
+            send(f"o_{k}", PP.at[j], RB.at[k - 1], hdev(k))
+    untwist(R0, 0, 2, 8)
+    arrive("s_gw", R1, sib)
+    untwist(R1, 512, 0, 4)
+    loads[3].wait()
+    total = RES[...].astype(F32) + PP[h].astype(F32)
+    for k in range(1, 8):
+        arrive(f"o_{k}", RB.at[k - 1], hdev(-k + 8))
+        total = total + RB[k - 1].astype(F32)
+    rounded = total.astype(BF)
+    att_out[...] = rounded
+    X[h, :, 0:512] = rounded
+
+    own = X.at[h, :, 0:512]
+    for k in range(1, 8):
+        send(f"x_{k}", own, own, hdev(k))
+    send("x_c", own, X.at[h, :, 512:1024], sib)
+    untwist(R1, 512, 4, 8)
+    for k in range(1, 8):
+        j = (h + 8 - k) % 8
+        arrive(f"x_{k}", X.at[j, :, 0:512], hdev(8 - k))
+        send(f"x_c{k}", X.at[j, :, 0:512], X.at[j, :, 512:1024], sib)
+    arrive("x_c", X.at[h, :, 512:1024], sib)
+    for k in range(1, 8):
+        j = (h + 8 - k) % 8
+        arrive(f"x_c{k}", X.at[j, :, 512:1024], sib)
+
+    def product(out, g, col0, width):
+        @pl.loop(0, width // 256)
+        def _(i):
+            rows = X[pl.ds(2 * g, 2)].reshape(256, 1024)
+            cols = pl.ds(pl.multiple_of(col0 + i * 256, 256), 256)
+            part = jnp.dot(rows, WC[:, cols], preferred_element_type=F32)
+            out[:, :, pl.ds(pl.multiple_of(i * 256, 256), 256)] = part.astype(BF).reshape(2, 128, 256)
+
+    groups = [(y + 3) % 4, (y + 1) % 4, (y + 2) % 4, y]
+    step_dev = [wdev(0, 1), wdev(0, 3)]
+    from_dev = [wdev(0, 3), wdev(0, 1)]
+    xdev = wdev(1, 0)
+    xo = 1 - xh
+
+    def first(d, s):
+        return (y + 3 - s + 4) % 4 if d == 0 else (y + 1 + s) % 4
+
+    def a_piece(d, gi):
+        g = groups[gi]
+        product(PA.at[d, g], g, d * A_W, A_W)
+
+    def b_piece(d, gi):
+        g = groups[gi]
+        product(PB.at[d, g], g, 2 * A_W + d * B_W, B_W)
+        send(f"bx_{d}{gi}", PB.at[d, g, xo], RBX.at[d, g], xdev)
+
+    a_piece(0, 0)
+    send("a_00", PA.at[0, groups[0]], RA.at[0, 0], step_dev[0])
+    a_piece(1, 1)
+    send("a_10", PA.at[1, groups[1]], RA.at[1, 0], step_dev[1])
+    b_piece(0, 0)
+    b_piece(1, 1)
+    b_piece(0, 2)
+    b_piece(1, 2)
+    a_piece(0, 2)
+    a_piece(1, 2)
+    b_piece(0, 1)
+    b_piece(1, 0)
+    b_piece(0, 3)
+    b_piece(1, 3)
+    a_piece(0, 1)
+    a_piece(1, 0)
+    a_piece(0, 3)
+    a_piece(1, 3)
+
+    ones = jnp.ones((8, 1024), BF)
+
+    @pl.loop(0, 8)
+    def _(b):
+        v = X[b].astype(F32)
+        SQ[b] = lax.dot_general(
+            ones, (v * v).astype(BF), (((1,), (1,)), ((), ())), preferred_element_type=F32
+        )
+
+    others = [(dx, dy) for dx in range(2) for dy in range(4) if (dx, dy) != (0, 0)]
+    for n, (dx, dy) in enumerate(others):
+        b = ((y + dy) % 4) * 2 + (xh + dx) % 2
+        send(f"q_{n}", SQ.at[b], SQR.at[n], wdev(dx, dy))
+
+    def add(out, left, right, rows):
+        @pl.loop(0, rows // 32)
+        def _(i):
+            r = pl.ds(pl.multiple_of(i * 32, 32), 32)
+            out[r, :] = (left[r, :].astype(F32) + right[r, :].astype(F32)).astype(BF)
+
+    def a_step(s):
+        for d in range(2):
+            g = first(d, s)
+            arrive(f"a_{d}{s - 1}", RA.at[d, s - 1], from_dev[d])
+            for e in range(2):
+                add(PA.at[d, g, e], PA.at[d, g, e], RA.at[d, s - 1, e], 128)
+            if s < 3:
+                send(f"a_{d}{s}", PA.at[d, g], RA.at[d, s], step_dev[d])
+            else:
+                send(f"ax_{d}", PA.at[d, y, xo], RAX.at[d], xdev)
+
+    def b_x(d, gi):
+        g = groups[gi]
+        arrive(f"bx_{d}{gi}", RBX.at[d, g], xdev)
+        add(PB.at[d, g, xh], PB.at[d, g, xh], RBX.at[d, g], 128)
+
+    def b_step(d, s):
+        g = first(d, s)
+        if s:
+            arrive(f"b_{d}{s - 1}", RBY.at[d, s - 1], from_dev[d])
+            add(PB.at[d, g, xh], PB.at[d, g, xh], RBY.at[d, s - 1], 128)
+        if s < 3:
+            send(f"b_{d}{s}", PB.at[d, g, xh], RBY.at[d, s], step_dev[d])
+
+    b_x(0, 0)
+    b_step(0, 0)
+    b_x(1, 1)
+    b_step(1, 0)
+    a_step(1)
+    b_x(0, 2)
+    b_step(0, 1)
+    b_x(1, 2)
+    b_step(1, 1)
+    a_step(2)
+    b_x(0, 1)
+    b_step(0, 2)
+    b_x(1, 0)
+    b_step(1, 2)
+    b_x(0, 3)
+    b_x(1, 3)
+
+    squares = SQ[y * 2 + xh]
+    for n, (dx, dy) in enumerate(others):
+        arrive(f"q_{n}", SQR.at[n], wdev((2 - dx) % 2, -dy))
+        squares = squares + SQR[n]
+    scale = lax.rsqrt(jnp.transpose(squares)[:, 0:1] / D + epsilon)
+
+    def gated(left, right, n, col0):
+        gate = (left[:, 0:n].astype(F32) + right[:, 0:n].astype(F32)) * scale
+        up = (left[:, n : 2 * n].astype(F32) + right[:, n : 2 * n].astype(F32)) * scale
+        H[y, xh, :, col0 : col0 + n] = (gate / (1.0 + jnp.exp(-gate)) * up).astype(BF)
+
+    def cols(part, d):
+        n = (A_U, B_U)[part]
+        o = H_OFF[2 * part + d]
+        return slice(o, o + n)
+
+    for d in range(2):
+        arrive(f"b_{d}2", RBY.at[d, 2], from_dev[d])
+        gated(PB.at[d, y, xh], RBY.at[d, 2], B_U, H_OFF[2 + d])
+        piece = H.at[y, xh, :, cols(1, d)]
+        send(f"hb_{d}0", piece, piece, step_dev[d])
+        send(f"hbx_{d}", piece, piece, xdev)
+
+    def hb_step(s):
+        for d in range(2):
+            g = first(d, s)
+            piece = H.at[g, xh, :, cols(1, d)]
+            arrive(f"hb_{d}{s}", piece, from_dev[d])
+            if s < 2:
+                send(f"hb_{d}{s + 1}", piece, piece, step_dev[d])
+            send(f"hbx_{d}{s}", piece, piece, xdev)
+
+    a_step(3)
+    hb_step(0)
+    hb_step(1)
+    hb_step(2)
+    for d in range(2):
+        arrive(f"ax_{d}", RAX.at[d], xdev)
+        gated(PA.at[d, y, xh], RAX.at[d], A_U, H_OFF[d])
+        piece = H.at[y, xh, :, cols(0, d)]
+        send(f"ha_o{d}0", piece, piece, step_dev[d])
+        send(f"hax_{d}", piece, piece, xdev)
+    for d in range(2):
+        piece = H.at[y, xo, :, cols(0, d)]
+        arrive(f"hax_{d}", piece, xdev)
+        send(f"ha_p{d}0", piece, piece, step_dev[d])
+
+    loads[2].wait()
+    arrive("s_dw", DD.at[1], sib)
+
+    def down(g):
+        for e, out in ((0, PDO), (1, PDS)):
+            @pl.loop(0, 2)
+            def _(i):
+                n = pl.ds(pl.multiple_of(i * 256, 256), 256)
+                rows = H[g].reshape(256, HALF)
+                part = jnp.dot(rows, DD[e, :, n], preferred_element_type=F32)
+                out[pl.ds(2 * g, 2), :, n] = part.astype(BF).reshape(2, 128, 256)
+
+    def share(name, g):
+        pair = pl.ds(2 * g, 2)
+        send(name, PDS.at[pair], PDI.at[pair], sib)
+
+    def ha_step(s):
+        for who, e in (("o", xh), ("p", xo)):
+            for d in range(2):
+                g = first(d, s)
+                piece = H.at[g, e, :, cols(0, d)]
+                arrive(f"ha_{who}{d}{s}", piece, from_dev[d])
+                if s < 2:
+                    send(f"ha_{who}{d}{s + 1}", piece, piece, step_dev[d])
+
+    def hb_partner(s):
+        for d in range(2):
+            g = y if s < 0 else first(d, s)
+            arrive(f"hbx_{d}" if s < 0 else f"hbx_{d}{s}", H.at[g, xo, :, cols(1, d)], xdev)
+
+    hb_partner(-1)
+    down(y)
+    share("d_0", y)
+    ha_step(0)
+    hb_partner(0)
+    ha_step(1)
+    hb_partner(1)
+    down(groups[2])
+    share("d_1", groups[2])
+    ha_step(2)
+    hb_partner(2)
+    down(groups[0])
+    share("d_2", groups[0])
+    down(groups[1])
+    share("d_3", groups[1])
+
+    for n, g in enumerate((y, groups[2], groups[0], groups[1])):
+        pair = pl.ds(2 * g, 2)
+        arrive(f"d_{n}", PDI.at[pair], sib)
+    for k in range(1, 9):
+        j = (h + k) % 8
+        add(PDO.at[j], PDO.at[j], PDI.at[j], 128)
+        if k < 8:
+            send(f"f_{k}", PDO.at[j], FR.at[k - 1], hdev(k))
+    total = PDO[h].astype(F32)
+    for k in range(1, 8):
+        arrive(f"f_{k}", FR.at[k - 1], hdev(8 - k))
+        total = total + FR[k - 1].astype(F32)
+    upd_out[...] = total.astype(BF)
+
+    for cp in sent:
+        cp.wait_send()
+
+
+N_COPIES = 140
+
+
+def layer(att, gate_up_weight, down_weight, out_weight, residual):
+    vm = pltpu.VMEM
+    scratch = [
+        vm((16, 64, 1024), BF),
+        vm((512, 2, HALF), BF),
+        vm((512, 2, HALF), BF),
+        vm((1024, 2 * HALF), BF),
+        vm((2, HALF, 512), BF),
+        vm((1024, 512), BF),
+        vm((128, 512), BF),
+        vm((8, 128, 512), BF),
+        vm((7, 128, 512), BF),
+        vm((8, 128, 1024), BF),
+        vm((2, 4, 2, 128, A_W), BF),
+        vm((2, 4, 2, 128, B_W), BF),
+        vm((2, 3, 2, 128, A_W), BF),
+        vm((2, 128, A_W), BF),
+        vm((2, 4, 128, B_W), BF),
+        vm((2, 3, 128, B_W), BF),
+        vm((8, 8, 128), F32),
+        vm((7, 8, 128), F32),
+        vm((4, 2, 128, HALF), BF),
+        vm((8, 128, 512), BF),
+        vm((8, 128, 512), BF),
+        vm((8, 128, 512), BF),
+        vm((7, 128, 512), BF),
+        pltpu.SemaphoreType.DMA((4,)),
+        pltpu.SemaphoreType.DMA((N_COPIES,)),
+        pltpu.SemaphoreType.DMA((N_COPIES,)),
+    ]
+    in_vmem = pl.BlockSpec(memory_space=pltpu.VMEM)
+    in_hbm = pl.BlockSpec(memory_space=pl.ANY)
+    return pl.pallas_call(
+        layer_kernel,
+        out_shape=(
+            jax.ShapeDtypeStruct((128, 512), BF),
+            jax.ShapeDtypeStruct((128, 512), BF),
+        ),
+        in_specs=[in_vmem, in_hbm, in_hbm, in_hbm, in_hbm],
+        out_specs=(in_vmem, in_vmem),
+        scratch_shapes=scratch,
+        name="layer",
+        compiler_params=pltpu.CompilerParams(
+            collective_id=0, has_side_effects=True, vmem_limit_bytes=60 << 20
+        ),
+    )(att, gate_up_weight, down_weight, out_weight, residual)
 
 
 def per_device(
@@ -90,38 +507,7 @@
         query_heads, cache_k, cache_v, tree_k, tree_v, context_len[0], tree_size[0], parents[0]
     )
     attention_rows = attention.reshape(node_count, kv_local * groups * HD).astype(jnp.bfloat16)
-    partial_value = jnp.dot(
-        lax.all_gather(attention_rows, "wide", axis=0, tiled=True),
-        out_weight,
-        preferred_element_type=jnp.float32,
-    )
-    projection = lax.psum(partial_value.astype(jnp.bfloat16), "head").astype(jnp.float32)
-    combined = residual.astype(jnp.float32) + projection
-    total_rows = combined.shape[0]
-    row_share = total_rows // lax.axis_size("head")
-    attended = lax.dynamic_slice_in_dim(
-        combined, lax.axis_index("head") * row_share, row_share, 0
-    ).astype(jnp.bfloat16)
-    squares = lax.psum(jnp.sum(combined * combined, axis=1), "wide")
-    normed = (combined * lax.rsqrt(squares[:, None] / D + epsilon)).astype(jnp.bfloat16)
-    width_local = gate_up_weight.shape[2]
-    stacked = gate_up_weight.reshape(gate_up_weight.shape[0], 2 * width_local)
-    summed = lax.psum_scatter(
-        jnp.dot(normed, stacked, preferred_element_type=jnp.float32).astype(jnp.bfloat16),
-        "wide",
-        scatter_dimension=0,
-        tiled=True,
-    ).astype(jnp.float32)
-    hidden = (jax.nn.silu(summed[:, :width_local]) * summed[:, width_local:]).astype(jnp.bfloat16)
-    down_part = jnp.dot(
-        lax.all_gather(hidden, "wide", axis=0, tiled=True),
-        down_weight,
-        preferred_element_type=jnp.float32,
-    )
-    update = lax.psum_scatter(
-        down_part.astype(jnp.bfloat16), "head", scatter_dimension=0, tiled=True
-    )
-    return (attended, update)
+    return layer(attention_rows, gate_up_weight, down_weight, out_weight, residual)
 
 
 def solution(mesh):

time: 446 us -> 201 us (0.45)
  waiting for transfers between devices: 356 us -> 0 us
  Pallas kernels: 0 us -> 183 us
  blocking collectives: 27.8 us -> 0 us
  matrix products: 31.5 us -> 6.13 us
  between operations: 15.4 us -> 2.26 us
  local copies, waits for them, and re-layouts: 9.44 us -> 4.34 us
    pallas_call x0 -> x1, Pallas kernels: none -> 183 us  [layer(): pl.pallas_call(layer_kernel, out_shape=(jax.ShapeDtypeStruct((128, 512),...]
    reduce_scatter x2 -> x0, waiting for transfers between devices: 171 us -> none  [the longest x1 134 us: per_device(): lax.psum_scatter(jnp.dot(normed, stacked, preferred_element_type=jnp.floa...]
    all_gather x2 -> x0, waiting for transfers between devices: 116 us -> none  [the longest x1 66.4 us: per_device(): lax.all_gather(hidden, 'wide', axis=0, tiled=True)]
    psum x1 -> x0, waiting for transfers between devices: 68.7 us -> none  [per_device(): lax.psum(partial_value.astype(jnp.bfloat16), 'head').astype(jnp.float32)]
    psum x1 -> x0, blocking collectives: 27.8 us -> none  [per_device(): squares = lax.psum(jnp.sum(combined * combined, axis=1), 'wide')]
    dot_general x3 -> x0, matrix products: 26.3 us -> none  [the longest x1 13.5 us: per_device(): jnp.dot(normed, stacked, preferred_element_type=jnp.float32)]
  transfers between devices with their start and end apart: 5 -> 0, of which waited for: 5 -> 0; matrix products, arithmetic and copies ran while one was open for 2% -> 0% of each run, Pallas kernels for 0% -> 0%
where the time goes in v1:
time: 201 us; the launch traced here: 199 us
  Pallas kernels  183 us (91%)
  matrix products  6.13 us (3%)
  local copies, waits for them, and re-layouts  4.34 us (2%)
  other arithmetic  3.36 us (2%)
  between operations  2.26 us (1%)
    pallas_call x1, Pallas kernels, layer(): pl.pallas_call(layer_kernel, out_shape=(jax.ShapeDtypeStruct((128, 512),...  183 us
    unnamed x17, local copies, waits for them, and re-layouts  4.16 us

profile of v1, /device:TPU:8, one launch (start us, length us, event | category | flops | bytes accessed | tf_op | source)
XLA Modules:
  0.0 198.7 jit_solution(14930315832009498958)
XLA Ops:
  0.6 0.0 copy-start
  0.6 0.0 copy-start.2
  0.7 0.0 copy-start.6
  0.7 0.0 copy-start.3
  1.4 0.3 copy-done
  1.7 3.6 %bitcast_reduce_fusion = (f32[8,64]{1,0:T(8,128)S(1)}, f32[2048,64,8]{0,1,2:T(8,128)}) fusion(pred[2048]{0:T(1024)(128)(4,1)S(1)} %iota_compare_fusion.3, bf16[1,2048,128]{2,1,0:T(8,128)(2,1)S(1)} %copy-done, bf16[64,1024]{1,0:T(8,128)(2,1)} %param.12), kind=kOutput, calls=%fused_computation.1 | convolution fusion | flops 271580672 | bytes 4853760 | tf_op jit(solution)/shard_map/tkgd,ckd->kgtc/dot_general | solution.py:50
  5.3 0.0 copy-start.4
  6.1 0.0 copy-done.6
  6.1 0.2 convolution_minimum_fusion.5
  6.3 0.2 convolution_minimum_fusion.4
  6.4 0.2 convolution_minimum_fusion.3
  6.6 0.2 convolution_minimum_fusion.2
  6.8 0.2 convolution_minimum_fusion.1
  6.9 0.2 fusion.11
  7.1 0.1 copy.15
  7.2 0.0 copy-done.2
  7.2 0.0 copy-done.3
  7.2 0.0 copy-start.1
  7.3 0.3 fusion.34
  7.5 3.3 %fusion.1 = f32[8,64]{1,0:T(8,128)S(1)} fusion(f32[2048,64,8]{0,1,2:T(8,128)} %get-tuple-element.3, f32[8,64]{1,0:T(8,128)S(1)} %max.9, pred[2048]{0:T(1024)(128)(4,1)S(1)} %iota_compare_fusion.3), kind=kLoop, calls=%fused_computation.4 | loop fusion | flops 4193792 | bytes 4200448 | tf_op jit(solution)/shard_map/reduce_sum | solution.py:62
  10.8 0.0 copy-start.5
  10.8 0.1 fusion.18
  10.9 0.0 copy-done.4
  10.9 0.0 copy-done.1
  10.9 1.0 fusion.4
  11.9 0.0 copy-done.5
  11.9 0.2 fusion.14
  12.2 0.1 copy.18
  12.3 0.7 copy.35
  13.0 182.6 %layer.1 = (bf16[128,512]{1,0:T(8,128)(2,1)}, bf16[128,512]{1,0:T(8,128)(2,1)}) custom-call(bf16[64,1024]{1,0:T(8,128)(2,1)} %bitcast.110, bf16[512,2,3584]{2,1,0:T(2,128)(2,1)} %gw.1, bf16[3584,512]{1,0:T(8,128)(2,1)} %dw.1, bf16[1024,512]{1,0:T(8,128)(2,1)} %wo_hbm.1, bf16[1024,512]{1,0:T(8,128)(2,1)} %res_hbm.1), custom_call_target="tpu_custom_call" | custom-call | tf_op jit(solution)/shard_map/layer/pallas_call | solution.py:468
  195.5 1.6 copy.40
  197.1 1.6 copy.41
  (4 shorter events, 0.0 us)
Async XLA Ops:
  0.6 1.1 copy-start
  0.6 6.6 %copy-start.2 = (bf16[64,1024]{1,0:T(8,128)(2,1)S(1)}, bf16[64,1024]{1,0:T(8,128)(2,1)}, u32[]{:S(2)}) copy-start(bf16[64,1024]{1,0:T(8,128)(2,1)} %param.12) | copy-start | bytes 393220
  0.7 5.4 %copy-start.6 = (s32[1,64]{1,0:T(1,128)S(1)}, s32[1,64]{1,0:T(1,128)}, u32[]{:S(2)}) copy-start(s32[1,64]{1,0:T(1,128)} %param.19) | copy-start | bytes 772
  0.7 6.6 %copy-start.3 = (bf16[64,128]{1,0:T(8,128)(2,1)S(1)}, bf16[64,128]{1,0:T(8,128)(2,1)}, u32[]{:S(2)}) copy-start(bf16[64,128]{1,0:T(8,128)(2,1)} %param.13) | copy-start | bytes 49156
  5.3 5.6 %copy-start.4 = (bf16[1,2048,128]{2,1,0:T(8,128)(2,1)S(1)}, bf16[1,2048,128]{2,1,0:T(8,128)(2,1)}, u32[]{:S(2)}) copy-start(bf16[1,2048,128]{2,1,0:T(8,128)(2,1)} %param.16) | copy-start | bytes 1572868
  7.2 3.7 %copy-start.1 = (f32[2048,64,8]{0,1,2:T(8,128)S(1)}, f32[2048,64,8]{0,1,2:T(8,128)}, u32[]{:S(2)}) copy-start(f32[2048,64,8]{0,1,2:T(8,128)} %get-tuple-element.3) | copy-start | bytes 12582916
  10.8 1.1 copy-start.5

commit v2 on v0

v2 whole, which is shorter than its diff:
```python
import math

import jax
import jax.numpy as jnp
from jax import lax
from jax.experimental import pallas as pl
from jax.experimental.pallas import tpu as pltpu
from jax.sharding import PartitionSpec as P

D = 8192
HD = 128
CTX = 2048
TREE = 64

epsilon = 1e-05

BF = jnp.bfloat16
F32 = jnp.float32
MESH = pl.DeviceIdType.MESH

A_U = 512
B_U = 384
A_W = 2 * A_U
B_W = 2 * B_U
HALF = 2 * A_U + 2 * B_U
H_OFF = (0, A_U, 2 * A_U, 2 * A_U + B_U)
OTHERS = ((0, 1), (0, 3), (1, 0), (0, 2), (1, 1), (1, 3), (1, 2))

ORDER = (
    "at0", "at1", "u0", "u1", "u2", "gf001", "gf002", "gf003", "gf010", "gf011", "gf012", "gf013",
    "gf103", "gf110", "u3", "gf101", "gf113", "u4", "u5", "gf102", "u6", "gf111", "u7", "gf112",
    "u8", "u9", "u10", "u11", "u12", "u13", "u14", "u15", "op0", "op1", "cm0", "cm1", "xf01",
    "xf02", "xf03", "xf04", "xf05", "xf06", "xf07", "xf11", "xf12", "xr0", "ga00", "xf13", "xf14",
    "xf15", "ga01", "xf16", "xf17", "gb00", "gb01", "xr1", "ga10", "ga11", "as001", "as011",
    "gb10", "gb11", "bs000", "sq0", "sq1", "as101", "bs010", "as111", "as002", "as012", "bs001",
    "bs011", "bs100", "as102", "as112", "bs110", "as003", "as013", "bs002", "bs012", "bs101",
    "sc0", "sc1", "af00", "as113", "as103", "bs111", "af01", "bf00", "hp009", "bf01", "bs102",
    "ho000", "bs112", "af11", "hb000", "ho010", "hp000", "hb010", "af10", "bf10", "bf11", "hp019",
    "ho001", "ho110", "dn00", "hb001", "hp119", "ho011", "hp001", "hb011", "ho100", "hb110",
    "fz00", "hb100", "hp010", "hp109", "ho111", "hb002", "dn10", "hp110", "ho101", "hb012",
    "hb101", "fz10", "hb111", "hp100", "hp011", "dn01", "hb102", "hp111", "hp101", "dn11", "hb112",
    "fz01", "dn02", "fz11", "dn12", "fz02", "fz12", "fo0", "fo1",
)


def layer_kernel(
    queries, fresh_k, fresh_v, parents, length, live, keys_hbm, values_hbm,
    gw, dw, wo_hbm, res_hbm,
    att_out, upd_out,
    KS, VS, FK, FV, S, PR, TB, ATT,
    G, R0, R1, WC, DD, WO, RES, PP, RB, X, PA, PB, RA, RAX, RBX, RBY, SQ, SQR, SC, H, PDO, PDS, PDI, FR,
    lsem, ssem, rsem,
):
    h = lax.axis_index("head")
    w = lax.axis_index("wide")
    xh = w // 8
    y = (w // 2) % 4
    c = w % 2
    flip = 1 - 2 * c
    xo = 1 - xh

    def wide(dxh, dy):
        return (((xh + dxh + 2) % 2) * 4 + (y + dy + 4) % 4) * 2 + c

    sib = (h, w + flip)

    def wdev(dxh, dy):
        return (h, wide(dxh, dy))

    def hdev(k):
        return ((h + k) % 8, w)

    names = {}
    sent = []

    def copy_of(i, src, dst, dev):
        return pltpu.make_async_remote_copy(
            src_ref=src, dst_ref=dst, send_sem=ssem.at[i], recv_sem=rsem.at[i],
            device_id=dev, device_id_type=MESH,
        )

    def send(name, src, dst, dev):
        assert name not in names
        i = names.setdefault(name, len(names))
        cp = copy_of(i, src, dst, dev)
        cp.start()
        sent.append(cp)

    def arrive(name, dst, dev):
        copy_of(names[name], dst, dst, dev).wait_recv()

    mine = pl.ds(pl.multiple_of(c * HALF, 128), HALF)
    other = pl.ds(pl.multiple_of((1 - c) * HALF, 128), HALF)
    loads = [
        pltpu.make_async_copy(keys_hbm.at[0], KS, lsem.at[0]),
        pltpu.make_async_copy(values_hbm.at[0], VS, lsem.at[1]),
        pltpu.make_async_copy(gw.at[:, :, mine], R0, lsem.at[2]),
        pltpu.make_async_copy(wo_hbm, WO, lsem.at[3]),
        pltpu.make_async_copy(
            res_hbm.at[pl.ds(pl.multiple_of(h * 128, 128), 128), :], RES, lsem.at[4]
        ),
        pltpu.make_async_copy(dw.at[mine, :], DD.at[0], lsem.at[5]),
    ]
    for cp in loads:
        cp.start()

    partners = [sib]
    partners += [wdev(dx, dy) for dx, dy in OTHERS]
    partners += [hdev(k) for k in range(1, 8)]
    barrier = pltpu.get_barrier_semaphore()
    for dev in partners:
        pl.semaphore_signal(barrier, inc=1, device_id=dev, device_id_type=MESH)

    node = lax.broadcasted_iota(jnp.int32, (TREE, TREE), 0)
    child = lax.broadcasted_iota(jnp.int32, (TREE, TREE), 1)
    linked = (parents[...] == node) | (node == child)
    reached = jnp.where(linked, 1.0, 0.0).astype(BF)
    for squaring in range(6):
        reached = jnp.minimum(jnp.dot(reached, reached, preferred_element_type=F32), 1.0).astype(BF)
    same = jnp.where(node == child, 1.0, 0.0).astype(BF)
    visible = lax.dot_general(reached, same, (((0,), (0,)), ((), ())), preferred_element_type=F32)
    TB[...] = jnp.full((TREE, 128), -1e30, F32)
    TB[:, 0:TREE] = jnp.where((visible > 0.5) & (child < live[0]), 0.0, -1e30)
    FK[0:TREE] = fresh_k[...]
    FK[TREE:128] = jnp.zeros((128 - TREE, HD), BF)
    FV[0:TREE] = fresh_v[...]
    FV[TREE:128] = jnp.zeros((128 - TREE, HD), BF)
    positions = lax.broadcasted_iota(jnp.int32, (1, CTX), 1)
    cache_bias = jnp.where(positions < length[0], 0.0, -1e30)
    score_scale = 1.0 / math.sqrt(HD)

    def attend(t):
        if t == 0:
            loads[0].wait()
        r0 = 32 * t
        q = jnp.concatenate([queries[r0 : r0 + 32, j * HD : (j + 1) * HD] for j in range(8)], axis=0)
        trans = (((1,), (1,)), ((), ()))

        @pl.loop(0, CTX // 512)
        def _(i):
            n = pl.ds(pl.multiple_of(i * 512, 512), 512)
            S[:, n] = lax.dot_general(q, KS[n, :], trans, preferred_element_type=F32)

        S[:, CTX : CTX + 128] = lax.dot_general(q, FK[...], trans, preferred_element_type=F32)
        if t == 0:
            loads[1].wait()
        tree_bias = TB[r0 : r0 + 32, :]
        alive = lax.broadcasted_iota(jnp.int32, (32, 1), 0) + r0 < live[0]
        denominators = []
        for j in range(8):
            r = slice(32 * j, 32 * j + 32)
            cache = S[r, 0:CTX] * score_scale + cache_bias
            tree = S[r, CTX : CTX + 128] * score_scale + tree_bias
            row_max = jnp.maximum(
                jnp.max(cache, axis=1, keepdims=True), jnp.max(tree, axis=1, keepdims=True)
            )
            cache = jnp.exp(cache - row_max)
            tree = jnp.exp(tree - row_max)
            denominators.append(
                jnp.sum(cache, axis=1, keepdims=True) + jnp.sum(tree, axis=1, keepdims=True)
            )
            PR[r, 0:CTX] = cache.astype(BF)
            PR[r, CTX : CTX + 128] = tree.astype(BF)
        out = jnp.dot(PR[:, 0:CTX], VS[...], preferred_element_type=F32)
        out = out + jnp.dot(PR[:, CTX : CTX + 128], FV[...], preferred_element_type=F32)
        for j in range(8):
            part = out[32 * j : 32 * j + 32] / denominators[j]
            ATT[t, :, j * HD : (j + 1) * HD] = jnp.where(alive, part, 0.0).astype(BF)
        if t == 0:
            pl.semaphore_wait(barrier, len(partners))
        for dx, dy in OTHERS:
            send(f"g{t}{dx}{dy}", ATT.at[t], G.at[t, w], wdev(dx, dy))
        send(f"gc{t}", ATT.at[t], G.at[t, w], sib)
        if t == 0:
            send("s_gw", gw.at[:, :, other], R1, sib)
            send("s_dw", dw.at[other, :], DD.at[1], sib)
        G[t, w] = ATT[t]

    def gather_on(t, dx, dy):
        src = wide(-dx, -dy)
        arrive(f"g{t}{dx}{dy}", G.at[t, src], wdev(-dx, -dy))
        send(f"gc{t}{dx}{dy}", G.at[t, src], G.at[t, src], sib)

    def untwist(k):
        if k == 0:
            loads[2].wait()
        if k == 8:
            arrive("s_gw", R1, sib)
        raw = R0 if k < 8 else R1
        i = k % 8
        b = raw[64 * i : 64 * i + 64]
        gate, up = b[:, 0, :], b[:, 1, :]
        o = slice(64 * k, 64 * k + 64)
        for p in range(4):
            n = A_U if p < 2 else B_U
            u = H_OFF[p]
            WC[o, 2 * u : 2 * u + n] = gate[:, u : u + n]
            WC[o, 2 * u + n : 2 * u + 2 * n] = up[:, u : u + n]

    def project(t):
        arrive(f"gc{t}", G.at[t, w + flip], sib)
        for dx, dy in OTHERS:
            arrive(f"gc{t}{dx}{dy}", G.at[t, wide(-dx, -dy) + flip], sib)
        if t == 0:
            loads[3].wait()
        rows = G[t].reshape(512, 1024)
        PP[t] = jnp.dot(rows, WO[...], preferred_element_type=F32).astype(BF).reshape(8, 64, 512)
        for k in range(1, 8):
            send(f"o{t}{k}", PP.at[t, (h + k) % 8], RB.at[t, k - 1], hdev(k))

    def combine(t):
        if t == 0:
            loads[4].wait()
        rows = (slice(32 * t, 32 * t + 32), slice(64 + 32 * t, 96 + 32 * t))
        total = PP[t, h].astype(F32) + jnp.concatenate([RES[r, :] for r in rows], axis=0).astype(F32)
        for k in range(1, 8):
            arrive(f"o{t}{k}", RB.at[t, k - 1], hdev(8 - k))
            total = total + RB[t, k - 1].astype(F32)
        rounded = total.astype(BF)
        X[t, h, :, 0:512] = rounded
        own = X.at[t, h, :, 0:512]
        for k in range(1, 8):
            send(f"x{t}{k}", own, own, hdev(k))
        send(f"xc{t}", own, X.at[t, h, :, 512:1024], sib)
        att_out[rows[0], :] = rounded[0:32]
        att_out[rows[1], :] = rounded[32:64]

    def spread(t, k):
        j = (h + 8 - k) % 8
        arrive(f"x{t}{k}", X.at[t, j, :, 0:512], hdev(8 - k))
        send(f"xc{t}{k}", X.at[t, j, :, 0:512], X.at[t, j, :, 512:1024], sib)

    def spread_end(t):
        arrive(f"xc{t}", X.at[t, h, :, 512:1024], sib)
        for k in range(1, 8):
            arrive(f"xc{t}{k}", X.at[t, (h + 8 - k) % 8, :, 512:1024], sib)

    step_dev = [wdev(0, 1), wdev(0, 3)]
    from_dev = [wdev(0, 3), wdev(0, 1)]
    xdev = wdev(1, 0)

    def first(d, s):
        return (y + 3 - s + 4) % 4 if d == 0 else (y + 1 + s) % 4

    def product(t, out, col0, width):
        @pl.loop(0, width // 256)
        def _(i):
            rows = X[t].reshape(512, 1024)
            cols = pl.ds(pl.multiple_of(col0 + i * 256, 256), 256)
            part = jnp.dot(rows, WC[:, cols], preferred_element_type=F32).astype(BF)
            out[:, :, :, pl.ds(pl.multiple_of(i * 256, 256), 256)] = part.reshape(4, 2, 64, 256)

    def a_piece(t, d):
        product(t, PA.at[t, d], d * A_W, A_W)
        send(f"a{t}{d}0", PA.at[t, d, first(d, 0)], RA.at[t, d, 0], step_dev[d])

    def b_piece(t, d):
        product(t, PB.at[t, d], 2 * A_W + d * B_W, B_W)
        for s in range(4):
            g = first(d, s)
            send(f"bx{t}{d}{s}", PB.at[t, d, g, xo], RBX.at[t, d, s], xdev)

    def squares(t):
        ones = jnp.ones((8, 1024), BF)
        for b in range(8):
            v = X[t, b].astype(F32)
            part = lax.dot_general(
                ones, (v * v).astype(BF), (((1,), (1,)), ((), ())), preferred_element_type=F32
            )
            SQ[t, b] = jnp.concatenate([part, part], axis=1)
        for n, (dx, dy) in enumerate(OTHERS):
            b = ((y + dy) % 4) * 2 + (xh + dx) % 2
            send(f"q{t}{n}", SQ.at[t, b], SQR.at[t, n], wdev(dx, dy))

    def row_scale(t):
        total = SQ[t, y * 2 + xh]
        for n, (dx, dy) in enumerate(OTHERS):
            arrive(f"q{t}{n}", SQR.at[t, n], wdev(-dx, -dy))
            total = total + SQR[t, n]
        scale = lax.rsqrt(jnp.transpose(total)[0:64, 0:1] / D + epsilon)
        SC[t] = jnp.broadcast_to(scale, (64, 128))

    def add(out, left, right):
        for i in range(2):
            r = slice(32 * i, 32 * i + 32)
            out[r, :] = (left[r, :].astype(F32) + right[r, :].astype(F32)).astype(BF)

    def a_step(t, d, s):
        g = first(d, s)
        arrive(f"a{t}{d}{s - 1}", RA.at[t, d, s - 1], from_dev[d])
        for e in range(2):
            add(PA.at[t, d, g, e], PA.at[t, d, g, e], RA.at[t, d, s - 1, e])
        if s < 3:
            send(f"a{t}{d}{s}", PA.at[t, d, g], RA.at[t, d, s], step_dev[d])
        else:
            send(f"xx{t}{d}", PA.at[t, d, y, xo], RAX.at[t, d], xdev)

    def b_sum(t, d, s):
        g = first(d, s)
        out = PB.at[t, d, g, xh]
        arrive(f"bx{t}{d}{s}", RBX.at[t, d, s], xdev)
        add(out, out, RBX.at[t, d, s])
        if s and s < 3:
            arrive(f"b{t}{d}{s - 1}", RBY.at[t, d, s - 1], from_dev[d])
            add(out, out, RBY.at[t, d, s - 1])
        if s < 3:
            send(f"b{t}{d}{s}", out, RBY.at[t, d, s], step_dev[d])

    def gated(t, left, right, n, col0):
        scale = SC[t, :, 0:1]
        gate = (left[:, 0:n].astype(F32) + right[:, 0:n].astype(F32)) * scale
        up = (left[:, n : 2 * n].astype(F32) + right[:, n : 2 * n].astype(F32)) * scale
        H[t, y, xh, :, col0 : col0 + n] = (gate / (1.0 + jnp.exp(-gate)) * up).astype(BF)

    def cols(part, d):
        o = H_OFF[2 * part + d]
        return slice(o, o + (A_U, B_U)[part])

    def b_end(t, d):
        b_sum(t, d, 3)
        arrive(f"b{t}{d}2", RBY.at[t, d, 2], from_dev[d])
        gated(t, PB.at[t, d, y, xh], RBY.at[t, d, 2], B_U, H_OFF[2 + d])
        piece = H.at[t, y, xh, :, cols(1, d)]
        send(f"hb{t}{d}0", piece, piece, step_dev[d])
        send(f"hx{t}{d}9", piece, piece, xdev)

    def hb_step(t, d, s):
        piece = H.at[t, first(d, s), xh, :, cols(1, d)]
        arrive(f"hb{t}{d}{s}", piece, from_dev[d])
        if s < 2:
            send(f"hb{t}{d}{s + 1}", piece, piece, step_dev[d])
        send(f"hx{t}{d}{s}", piece, piece, xdev)

    def a_end(t, d):
        arrive(f"xx{t}{d}", RAX.at[t, d], xdev)
        gated(t, PA.at[t, d, y, xh], RAX.at[t, d], A_U, H_OFF[d])
        piece = H.at[t, y, xh, :, cols(0, d)]
        send(f"ho{t}{d}0", piece, piece, step_dev[d])
        send(f"hp{t}{d}9", piece, piece, xdev)

    def ha_step(t, d, s, q):
        if s == 9:
            piece = H.at[t, y, xo, :, cols(0, d)]
            arrive(f"hp{t}{d}9", piece, xdev)
            send(f"hp{t}{d}0", piece, piece, step_dev[d])
            return
        piece = H.at[t, first(d, s), xh if q == "o" else xo, :, cols(0, d)]
        arrive(f"h{q}{t}{d}{s}", piece, from_dev[d])
        if s < 2:
            send(f"h{q}{t}{d}{s + 1}", piece, piece, step_dev[d])

    down_ready = []

    def down(t, i):
        if not down_ready:
            loads[5].wait()
            arrive("s_dw", DD.at[1], sib)
            down_ready.append(True)
        steps = ((9,), (1,), (0, 2))[i]
        for s in steps:
            for d in range(2):
                g = y if s == 9 else first(d, s)
                arrive(f"hx{t}{d}{s}", H.at[t, g, xo, :, cols(1, d)], xdev)
                if s == 2:
                    ha_step(t, d, 2, "o")
                    ha_step(t, d, 2, "p")
        gs = ((y,), ((y + 2) % 4,), ((y + 1) % 4, (y + 3) % 4))[i]
        for e, out in ((1, PDS), (0, PDO)):
            @pl.loop(0, 2)
            def _(n):
                n = pl.ds(pl.multiple_of(n * 256, 256), 256)
                rows = jnp.concatenate([H[t, g].reshape(128, HALF) for g in gs], axis=0)
                part = jnp.dot(rows, DD[e, :, n], preferred_element_type=F32).astype(BF)
                for m, g in enumerate(gs):
                    out[t, pl.ds(2 * g, 2), :, n] = part[128 * m : 128 * m + 128].reshape(2, 64, 256)

            if e:
                for m, g in enumerate(gs):
                    pair = pl.ds(2 * g, 2)
                    send(f"sh{t}{i}{m}", PDS.at[t, pair], PDI.at[t, pair], sib)

    def share(t, i):
        gs = ((y,), ((y + 2) % 4,), ((y + 1) % 4, (y + 3) % 4))[i]
        for k in range(1, 8):
            names.setdefault(f"f{t}{k}", len(names))
        base = names[f"f{t}1"]
        for m, g in enumerate(gs):
            pair = pl.ds(2 * g, 2)
            arrive(f"sh{t}{i}{m}", PDI.at[t, pair], sib)
            for e in range(2):
                j = 2 * g + e
                k = (j - h + 8) % 8
                add(PDO.at[t, j], PDO.at[t, j], PDI.at[t, j])

                @pl.when(k != 0)
                def _():
                    copy_of(base + k - 1, PDO.at[t, j], FR.at[t, k - 1], (j, w)).start()

    def finish(t):
        total = PDO[t, h].astype(F32)
        for k in range(1, 8):
            arrive(f"f{t}{k}", FR.at[t, k - 1], hdev(8 - k))
            total = total + FR[t, k - 1].astype(F32)
            sent.append(copy_of(names[f"f{t}{k}"], PDO.at[t, (h + k) % 8], FR.at[t, k - 1], hdev(k)))
        rounded = total.astype(BF)
        upd_out[32 * t : 32 * t + 32, :] = rounded[0:32]
        upd_out[64 + 32 * t : 96 + 32 * t, :] = rounded[32:64]

    steps = {}
    for k in range(16):
        steps[f"u{k}"] = (untwist, k)
    for t in range(2):
        steps[f"at{t}"] = (attend, t)
        for dx, dy in OTHERS:
            steps[f"gf{t}{dx}{dy}"] = (gather_on, t, dx, dy)
        steps[f"op{t}"] = (project, t)
        steps[f"cm{t}"] = (combine, t)
        for k in range(1, 8):
            steps[f"xf{t}{k}"] = (spread, t, k)
        steps[f"xr{t}"] = (spread_end, t)
        steps[f"sq{t}"] = (squares, t)
        steps[f"sc{t}"] = (row_scale, t)
        for d in range(2):
            steps[f"ga{t}{d}"] = (a_piece, t, d)
            steps[f"gb{t}{d}"] = (b_piece, t, d)
            for s in range(3):
                steps[f"as{t}{d}{s + 1}"] = (a_step, t, d, s + 1)
                steps[f"bs{t}{d}{s}"] = (b_sum, t, d, s)
                steps[f"hb{t}{d}{s}"] = (hb_step, t, d, s)
            steps[f"bf{t}{d}"] = (b_end, t, d)
            steps[f"af{t}{d}"] = (a_end, t, d)
            for s in (0, 1):
                for q in "op":
                    steps[f"h{q}{t}{d}{s}"] = (ha_step, t, d, s, q)
            steps[f"hp{t}{d}9"] = (ha_step, t, d, 9, "p")
        for i in range(3):
            steps[f"dn{t}{i}"] = (down, t, i)
            steps[f"fz{t}{i}"] = (share, t, i)
        steps[f"fo{t}"] = (finish, t)
    assert sorted(steps) == sorted(ORDER)
    for name in ORDER:
        step, *where = steps[name]
        step(*where)

    assert len(names) <= N_COPIES
    for cp in sent:
        cp.wait_send()


N_COPIES = 232


def layer(
    queries, fresh_keys, fresh_values, cached_keys, cached_values, context_len, tree_size, parents,
    residual, out_weight, gate_up_weight, down_weight,
):
    vm = pltpu.VMEM
    scratch = [
        vm((CTX, HD), BF),
        vm((CTX, HD), BF),
        vm((128, HD), BF),
        vm((128, HD), BF),
        vm((256, CTX + 128), F32),
        vm((256, CTX + 128), BF),
        vm((TREE, 128), F32),
        vm((2, 32, 1024), BF),
        vm((2, 16, 32, 1024), BF),
        vm((512, 2, HALF), BF),
        vm((512, 2, HALF), BF),
        vm((1024, 2 * HALF), BF),
        vm((2, HALF, 512), BF),
        vm((1024, 512), BF),
        vm((128, 512), BF),
        vm((2, 8, 64, 512), BF),
        vm((2, 7, 64, 512), BF),
        vm((2, 8, 64, 1024), BF),
        vm((2, 2, 4, 2, 64, A_W), BF),
        vm((2, 2, 4, 2, 64, B_W), BF),
        vm((2, 2, 3, 2, 64, A_W), BF),
        vm((2, 2, 64, A_W), BF),
        vm((2, 2, 4, 64, B_W), BF),
        vm((2, 2, 3, 64, B_W), BF),
        vm((2, 8, 8, 128), F32),
        vm((2, 7, 8, 128), F32),
        vm((2, 64, 128), F32),
        vm((2, 4, 2, 64, HALF), BF),
        vm((2, 8, 64, 512), BF),
        vm((2, 8, 64, 512), BF),
        vm((2, 8, 64, 512), BF),
        vm((2, 7, 64, 512), BF),
        pltpu.SemaphoreType.DMA((6,)),
        pltpu.SemaphoreType.DMA((N_COPIES,)),
        pltpu.SemaphoreType.DMA((N_COPIES,)),
    ]
    in_vmem = pl.BlockSpec(memory_space=pltpu.VMEM)
    in_smem = pl.BlockSpec(memory_space=pltpu.SMEM)
    in_hbm = pl.BlockSpec(memory_space=pl.ANY)
    return pl.pallas_call(
        layer_kernel,
        out_shape=(
            jax.ShapeDtypeStruct((128, 512), BF),
            jax.ShapeDtypeStruct((128, 512), BF),
        ),
        in_specs=[in_vmem] * 4 + [in_smem] * 2 + [in_hbm] * 6,
        out_specs=(in_vmem, in_vmem),
        scratch_shapes=scratch,
        name="layer",
        compiler_params=pltpu.CompilerParams(
            collective_id=0, has_side_effects=True, vmem_limit_bytes=60 << 20
        ),
    )(
        queries, fresh_keys, fresh_values, parents, context_len, tree_size, cached_keys, cached_values,
        gate_up_weight, down_weight, out_weight, residual,
    )


def solution(mesh):
    placed = (
        P("wide", "head"),
        P("wide", "head"),
        P("wide", "head"),
        P("wide", None, "head"),
        P("wide", None, "head"),
        P("wide"),
        P("wide"),
        P("wide", None),
        P(None, "wide"),
        P("head", "wide"),
        P("wide", None, "head"),
        P("head", "wide"),
    )
    return jax.shard_map(
        layer,
        mesh=mesh,
        in_specs=placed,
        out_specs=(P("head", "wide"), P("head", "wide")),
        check_vma=False,
    )
```

time: 446 us -> 162 us (0.36)
  waiting for transfers between devices: 356 us -> 0 us
  Pallas kernels: 0 us -> 156 us
  matrix products: 31.5 us -> 0 us
  blocking collectives: 27.8 us -> 0 us
  between operations: 15.4 us -> 1.93 us
  local copies, waits for them, and re-layouts: 9.44 us -> 3.14 us
  other arithmetic: 5.26 us -> 0 us
    reduce_scatter x2 -> x0, waiting for transfers between devices: 171 us -> none  [the longest x1 134 us: per_device(): lax.psum_scatter(jnp.dot(normed, stacked, preferred_element_type=jnp.floa...]
    pallas_call x0 -> x1, Pallas kernels: none -> 156 us  [layer(): pl.pallas_call(layer_kernel, out_shape=(jax.ShapeDtypeStruct((128, 512),...]
    all_gather x2 -> x0, waiting for transfers between devices: 116 us -> none  [the longest x1 66.4 us: per_device(): lax.all_gather(hidden, 'wide', axis=0, tiled=True)]
    psum x1 -> x0, waiting for transfers between devices: 68.7 us -> none  [per_device(): lax.psum(partial_value.astype(jnp.bfloat16), 'head').astype(jnp.float32)]
    dot_general x13 -> x0, matrix products: 31.5 us -> none  [the longest x1 13.5 us: per_device(): jnp.dot(normed, stacked, preferred_element_type=jnp.float32)]
    psum x1 -> x0, blocking collectives: 27.8 us -> none  [per_device(): squares = lax.psum(jnp.sum(combined * combined, axis=1), 'wide')]
    unnamed x16 -> x2, local copies, waits for them, and re-layouts: 8.58 us -> 3.14 us
  transfers between devices with their start and end apart: 5 -> 0, of which waited for: 5 -> 0; matrix products, arithmetic and copies ran while one was open for 2% -> 0% of each run, Pallas kernels for 0% -> 0%
where the time goes in v2:
time: 162 us; the launch traced here: 161 us
  Pallas kernels  156 us (96%)
  local copies, waits for them, and re-layouts  3.14 us (2%)
  between operations  1.93 us (1%)
    pallas_call x1, Pallas kernels, layer(): pl.pallas_call(layer_kernel, out_shape=(jax.ShapeDtypeStruct((128, 512),...  156 us

profile of v2, /device:TPU:8, one launch (start us, length us, event | category | flops | bytes accessed | tf_op | source)
XLA Modules:
  0.0 161.4 jit_solution(17186954226777063161)
XLA Ops:
  1.9 156.3 %layer.1 = (bf16[128,512]{1,0:T(8,128)(2,1)}, bf16[128,512]{1,0:T(8,128)(2,1)}) custom-call(bf16[64,1024]{1,0:T(8,128)(2,1)} %queries.1, bf16[64,128]{1,0:T(8,128)(2,1)} %fresh_k.1, bf16[64,128]{1,0:T(8,128)(2,1)} %fresh_v.1, s32[1,64]{1,0:T(1,128)} %parents.1, s32[1]{0:T(128)S(6)} %copy.16.length, s32[1]{0:T(128)S(6)} %copy.17.live, ...), custom_call_target="tpu_custom_call" | custom-call | tf_op jit(solution)/shard_map/layer/pallas_call | solution.py:498
  158.3 1.6 copy.18
  159.8 1.6 copy.19

commit v3 on v2

--- a/solution.py
+++ b/solution.py
@@ -27,28 +27,28 @@
 OTHERS = ((0, 1), (0, 3), (1, 0), (0, 2), (1, 1), (1, 3), (1, 2))
 
 ORDER = (
-    "at0", "at1", "u0", "u1", "u2", "gf001", "gf002", "gf003", "gf010", "gf011", "gf012", "gf013",
-    "gf103", "gf110", "u3", "gf101", "gf113", "u4", "u5", "gf102", "u6", "gf111", "u7", "gf112",
-    "u8", "u9", "u10", "u11", "u12", "u13", "u14", "u15", "op0", "op1", "cm0", "cm1", "xf01",
-    "xf02", "xf03", "xf04", "xf05", "xf06", "xf07", "xf11", "xf12", "xr0", "ga00", "xf13", "xf14",
-    "xf15", "ga01", "xf16", "xf17", "gb00", "gb01", "xr1", "ga10", "ga11", "as001", "as011",
-    "gb10", "gb11", "bs000", "sq0", "sq1", "as101", "bs010", "as111", "as002", "as012", "bs001",
-    "bs011", "bs100", "as102", "as112", "bs110", "as003", "as013", "bs002", "bs012", "bs101",
-    "sc0", "sc1", "af00", "as113", "as103", "bs111", "af01", "bf00", "hp009", "bf01", "bs102",
-    "ho000", "bs112", "af11", "hb000", "ho010", "hp000", "hb010", "af10", "bf10", "bf11", "hp019",
-    "ho001", "ho110", "dn00", "hb001", "hp119", "ho011", "hp001", "hb011", "ho100", "hb110",
-    "fz00", "hb100", "hp010", "hp109", "ho111", "hb002", "dn10", "hp110", "ho101", "hb012",
-    "hb101", "fz10", "hb111", "hp100", "hp011", "dn01", "hb102", "hp111", "hp101", "dn11", "hb112",
-    "fz01", "dn02", "fz11", "dn12", "fz02", "fz12", "fo0", "fo1",
+    "in", "at0", "at1", "u0", "u1", "u2", "gf003", "gf001", "u3", "u4", "gf002", "gf011", "gf012",
+    "gf013", "gf010", "u5", "gf103", "u6", "op0", "gf111", "gf101", "gf110", "gf102", "gf113",
+    "u7", "gf112", "u8", "u9", "op1", "u10", "u11", "u12", "cm0", "u13", "u14", "u15", "cm1",
+    "xf01", "xf03", "xf02", "xf04", "xf05", "xf07", "xf06", "xf11", "xr0", "ga00", "xf13", "xf15",
+    "xf12", "ga01", "gb01", "gb00", "xf17", "xf16", "xf14", "sq0", "as001", "bs010", "xr1", "ga11",
+    "as011", "ga10", "bs011", "gb11", "gb10", "as002", "sq1", "bs000", "as111", "as101", "sc0",
+    "as012", "bs110", "bs012", "as003", "bs001", "as112", "bs100", "as102", "bs002", "as013",
+    "bs101", "bs111", "sc1", "bf01", "af00", "as103", "af01", "bf00", "as113", "hp009", "bs102",
+    "bs112", "hb010", "ho000", "hb000", "af10", "ho010", "hp000", "hp019", "bf11", "dn00", "bf10",
+    "ho011", "hb011", "ho001", "af11", "hb001", "hp010", "fz00", "hb110", "ho100", "hp001",
+    "hp109", "hb012", "hb100", "ho110", "hb002", "hp011", "hp119", "dn10", "hb111", "ho101",
+    "ho111", "dn01", "hp100", "fz10", "hb101", "hp110", "fz01", "dn02", "hb112", "hp101", "hb102",
+    "hp111", "dn11", "fz02", "dn12", "fz11", "fx0", "fz12", "fo0", "fx1", "fo1",
 )
 
 
 def layer_kernel(
     queries, fresh_k, fresh_v, parents, length, live, keys_hbm, values_hbm,
     gw, dw, wo_hbm, res_hbm,
-    att_out, upd_out,
+    out,
     KS, VS, FK, FV, S, PR, TB, ATT,
-    G, R0, R1, WC, DD, WO, RES, PP, RB, X, PA, PB, RA, RAX, RBX, RBY, SQ, SQR, SC, H, PDO, PDS, PDI, FR,
+    G, R0, R1, WC, DD, WO, RES, PP, RB, X, PA, PB, RA, RAX, RBX, RBY, SQ, SQR, SC, H, PDO, PDS, PDI, FR, FS, FXR,
     lsem, ssem, rsem,
 ):
     h = lax.axis_index("head")
@@ -63,6 +63,11 @@
         return (((xh + dxh + 2) % 2) * 4 + (y + dy + 4) % 4) * 2 + c
 
     sib = (h, w + flip)
+    xl = h // 4
+    z = h % 4
+
+    def place(j):
+        return 2 * (j % 4) + j // 4
 
     def wdev(dxh, dy):
         return (h, wide(dxh, dy))
@@ -75,12 +80,11 @@
 
     def copy_of(i, src, dst, dev):
         return pltpu.make_async_remote_copy(
-            src_ref=src, dst_ref=dst, send_sem=ssem.at[i], recv_sem=rsem.at[i],
+            src_ref=src, dst_ref=dst, send_sem=ssem.at[0], recv_sem=rsem.at[i],
             device_id=dev, device_id_type=MESH,
         )
 
     def send(name, src, dst, dev):
-        assert name not in names
         i = names.setdefault(name, len(names))
         cp = copy_of(i, src, dst, dev)
         cp.start()
@@ -110,6 +114,10 @@
     barrier = pltpu.get_barrier_semaphore()
     for dev in partners:
         pl.semaphore_signal(barrier, inc=1, device_id=dev, device_id_type=MESH)
+
+    def enter():
+        pl.semaphore_wait(barrier, len(partners))
+        send("s_gw", gw.at[:, :, other], R1, sib)
 
     node = lax.broadcasted_iota(jnp.int32, (TREE, TREE), 0)
     child = lax.broadcasted_iota(jnp.int32, (TREE, TREE), 1)
@@ -127,7 +135,7 @@
     FV[TREE:128] = jnp.zeros((128 - TREE, HD), BF)
     positions = lax.broadcasted_iota(jnp.int32, (1, CTX), 1)
     cache_bias = jnp.where(positions < length[0], 0.0, -1e30)
-    score_scale = 1.0 / math.sqrt(HD)
+    score_scale = math.log2(math.e) / math.sqrt(HD)
 
     def attend(t):
         if t == 0:
@@ -144,42 +152,38 @@
         S[:, CTX : CTX + 128] = lax.dot_general(q, FK[...], trans, preferred_element_type=F32)
         if t == 0:
             loads[1].wait()
-        tree_bias = TB[r0 : r0 + 32, :]
         alive = lax.broadcasted_iota(jnp.int32, (32, 1), 0) + r0 < live[0]
         denominators = []
-        for j in range(8):
-            r = slice(32 * j, 32 * j + 32)
-            cache = S[r, 0:CTX] * score_scale + cache_bias
-            tree = S[r, CTX : CTX + 128] * score_scale + tree_bias
+        for j in range(16):
+            r = slice(16 * j, 16 * j + 16)
+            n0 = r0 + 16 * (j % 2)
+            cache = S[r, 0:CTX] + cache_bias
+            tree = S[r, CTX : CTX + 128] + TB[n0 : n0 + 16, :]
             row_max = jnp.maximum(
                 jnp.max(cache, axis=1, keepdims=True), jnp.max(tree, axis=1, keepdims=True)
             )
-            cache = jnp.exp(cache - row_max)
-            tree = jnp.exp(tree - row_max)
+            cache = jnp.exp2((cache - row_max) * score_scale)
+            tree = jnp.exp2((tree - row_max) * score_scale)
             denominators.append(
                 jnp.sum(cache, axis=1, keepdims=True) + jnp.sum(tree, axis=1, keepdims=True)
             )
             PR[r, 0:CTX] = cache.astype(BF)
             PR[r, CTX : CTX + 128] = tree.astype(BF)
-        out = jnp.dot(PR[:, 0:CTX], VS[...], preferred_element_type=F32)
-        out = out + jnp.dot(PR[:, CTX : CTX + 128], FV[...], preferred_element_type=F32)
+        mixed = jnp.dot(PR[:, 0:CTX], VS[...], preferred_element_type=F32)
+        mixed = mixed + jnp.dot(PR[:, CTX : CTX + 128], FV[...], preferred_element_type=F32)
         for j in range(8):
-            part = out[32 * j : 32 * j + 32] / denominators[j]
+            below = jnp.concatenate(denominators[2 * j : 2 * j + 2], axis=0)
+            part = mixed[32 * j : 32 * j + 32] / below
             ATT[t, :, j * HD : (j + 1) * HD] = jnp.where(alive, part, 0.0).astype(BF)
-        if t == 0:
-            pl.semaphore_wait(barrier, len(partners))
         for dx, dy in OTHERS:
             send(f"g{t}{dx}{dy}", ATT.at[t], G.at[t, w], wdev(dx, dy))
         send(f"gc{t}", ATT.at[t], G.at[t, w], sib)
-        if t == 0:
-            send("s_gw", gw.at[:, :, other], R1, sib)
-            send("s_dw", dw.at[other, :], DD.at[1], sib)
         G[t, w] = ATT[t]
 
     def gather_on(t, dx, dy):
         src = wide(-dx, -dy)
         arrive(f"g{t}{dx}{dy}", G.at[t, src], wdev(-dx, -dy))
-        send(f"gc{t}{dx}{dy}", G.at[t, src], G.at[t, src], sib)
+        send(f"gc{t}", G.at[t, src], G.at[t, src], sib)
 
     def untwist(k):
         if k == 0:
@@ -198,42 +202,40 @@
             WC[o, 2 * u + n : 2 * u + 2 * n] = up[:, u : u + n]
 
     def project(t):
-        arrive(f"gc{t}", G.at[t, w + flip], sib)
-        for dx, dy in OTHERS:
-            arrive(f"gc{t}{dx}{dy}", G.at[t, wide(-dx, -dy) + flip], sib)
+        arrive(f"gc{t}", G.at[t, 0:8], sib)
         if t == 0:
             loads[3].wait()
         rows = G[t].reshape(512, 1024)
         PP[t] = jnp.dot(rows, WO[...], preferred_element_type=F32).astype(BF).reshape(8, 64, 512)
+        if t == 1:
+            send("s_dw", dw.at[other, :], DD.at[1], sib)
         for k in range(1, 8):
-            send(f"o{t}{k}", PP.at[t, (h + k) % 8], RB.at[t, k - 1], hdev(k))
+            send(f"o{t}", PP.at[t, (h + k) % 8], RB.at[t, k - 1], hdev(k))
 
     def combine(t):
         if t == 0:
             loads[4].wait()
         rows = (slice(32 * t, 32 * t + 32), slice(64 + 32 * t, 96 + 32 * t))
         total = PP[t, h].astype(F32) + jnp.concatenate([RES[r, :] for r in rows], axis=0).astype(F32)
-        for k in range(1, 8):
-            arrive(f"o{t}{k}", RB.at[t, k - 1], hdev(8 - k))
-            total = total + RB[t, k - 1].astype(F32)
+        arrive(f"o{t}", RB.at[t], hdev(1))
+        for k in range(7):
+            total = total + RB[t, k].astype(F32)
         rounded = total.astype(BF)
-        X[t, h, :, 0:512] = rounded
-        own = X.at[t, h, :, 0:512]
+        own = X.at[t, place(h), :, 0:512]
+        own[...] = rounded
         for k in range(1, 8):
             send(f"x{t}{k}", own, own, hdev(k))
-        send(f"xc{t}", own, X.at[t, h, :, 512:1024], sib)
-        att_out[rows[0], :] = rounded[0:32]
-        att_out[rows[1], :] = rounded[32:64]
+        send(f"xc{t}", own, X.at[t, place(h), :, 512:1024], sib)
+        out[0, rows[0], :] = rounded[0:32]
+        out[0, rows[1], :] = rounded[32:64]
 
     def spread(t, k):
-        j = (h + 8 - k) % 8
+        j = place((h + 8 - k) % 8)
         arrive(f"x{t}{k}", X.at[t, j, :, 0:512], hdev(8 - k))
-        send(f"xc{t}{k}", X.at[t, j, :, 0:512], X.at[t, j, :, 512:1024], sib)
+        send(f"xc{t}", X.at[t, j, :, 0:512], X.at[t, j, :, 512:1024], sib)
 
     def spread_end(t):
-        arrive(f"xc{t}", X.at[t, h, :, 512:1024], sib)
-        for k in range(1, 8):
-            arrive(f"xc{t}{k}", X.at[t, (h + 8 - k) % 8, :, 512:1024], sib)
+        arrive(f"xc{t}", X.at[t, :, :, 512:1024], sib)
 
     step_dev = [wdev(0, 1), wdev(0, 3)]
     from_dev = [wdev(0, 3), wdev(0, 1)]
@@ -270,12 +272,12 @@
             SQ[t, b] = jnp.concatenate([part, part], axis=1)
         for n, (dx, dy) in enumerate(OTHERS):
             b = ((y + dy) % 4) * 2 + (xh + dx) % 2
-            send(f"q{t}{n}", SQ.at[t, b], SQR.at[t, n], wdev(dx, dy))
+            send(f"q{t}", SQ.at[t, b], SQR.at[t, n], wdev(dx, dy))
 
     def row_scale(t):
         total = SQ[t, y * 2 + xh]
-        for n, (dx, dy) in enumerate(OTHERS):
-            arrive(f"q{t}{n}", SQR.at[t, n], wdev(-dx, -dy))
+        arrive(f"q{t}", SQR.at[t], wdev(0, 1))
+        for n in range(7):
             total = total + SQR[t, n]
         scale = lax.rsqrt(jnp.transpose(total)[0:64, 0:1] / D + epsilon)
         SC[t] = jnp.broadcast_to(scale, (64, 128))
@@ -381,32 +383,44 @@
 
     def share(t, i):
         gs = ((y,), ((y + 2) % 4,), ((y + 1) % 4, (y + 3) % 4))[i]
-        for k in range(1, 8):
-            names.setdefault(f"f{t}{k}", len(names))
-        base = names[f"f{t}1"]
+        index = names.setdefault(f"f{t}", len(names))
         for m, g in enumerate(gs):
             pair = pl.ds(2 * g, 2)
             arrive(f"sh{t}{i}{m}", PDI.at[t, pair], sib)
             for e in range(2):
                 j = 2 * g + e
-                k = (j - h + 8) % 8
                 add(PDO.at[t, j], PDO.at[t, j], PDI.at[t, j])
 
-                @pl.when(k != 0)
-                def _():
-                    copy_of(base + k - 1, PDO.at[t, j], FR.at[t, k - 1], (j, w)).start()
+            @pl.when(g != z)
+            def _():
+                slot = (g - z + 4) % 4 - 1
+                copy_of(index, PDO.at[t, pair], FR.at[t, slot], (xl * 4 + g, w)).start()
+
+    def head_sum(t, e):
+        total = PDO[t, 2 * z + e].astype(F32)
+        for n in range(3):
+            total = total + FR[t, n, e].astype(F32)
+        return total
+
+    def across(t):
+        arrive(f"f{t}", FR.at[t], hdev(1))
+        for n in range(1, 4):
+            g = (z + n) % 4
+            sent.append(
+                copy_of(names[f"f{t}"], PDO.at[t, pl.ds(2 * g, 2)], FR.at[t, n - 1], (xl * 4 + g, w))
+            )
+        FS[t] = head_sum(t, 1 - xl).astype(BF)
+        send(f"fx{t}", FS.at[t], FXR.at[t], hdev(4))
 
     def finish(t):
-        total = PDO[t, h].astype(F32)
-        for k in range(1, 8):
-            arrive(f"f{t}{k}", FR.at[t, k - 1], hdev(8 - k))
-            total = total + FR[t, k - 1].astype(F32)
-            sent.append(copy_of(names[f"f{t}{k}"], PDO.at[t, (h + k) % 8], FR.at[t, k - 1], hdev(k)))
+        total = head_sum(t, xl)
+        arrive(f"fx{t}", FXR.at[t], hdev(4))
+        total = total + FXR[t].astype(F32)
         rounded = total.astype(BF)
-        upd_out[32 * t : 32 * t + 32, :] = rounded[0:32]
-        upd_out[64 + 32 * t : 96 + 32 * t, :] = rounded[32:64]
-
-    steps = {}
+        out[1, 32 * t : 32 * t + 32, :] = rounded[0:32]
+        out[1, 64 + 32 * t : 96 + 32 * t, :] = rounded[32:64]
+
+    steps = {"in": (enter,)}
     for k in range(16):
         steps[f"u{k}"] = (untwist, k)
     for t in range(2):
@@ -436,8 +450,10 @@
         for i in range(3):
             steps[f"dn{t}{i}"] = (down, t, i)
             steps[f"fz{t}{i}"] = (share, t, i)
+        steps[f"fx{t}"] = (across, t)
         steps[f"fo{t}"] = (finish, t)
     assert sorted(steps) == sorted(ORDER)
+    assert len(ORDER) == len(set(ORDER))
     for name in ORDER:
         step, *where = steps[name]
         step(*where)
@@ -447,7 +463,7 @@
         cp.wait_send()
 
 
-N_COPIES = 232
+N_COPIES = 160
 
 
 def layer(
@@ -487,22 +503,21 @@
         vm((2, 8, 64, 512), BF),
         vm((2, 8, 64, 512), BF),
         vm((2, 8, 64, 512), BF),
-        vm((2, 7, 64, 512), BF),
+        vm((2, 3, 2, 64, 512), BF),
+        vm((2, 64, 512), BF),
+        vm((2, 64, 512), BF),
         pltpu.SemaphoreType.DMA((6,)),
-        pltpu.SemaphoreType.DMA((N_COPIES,)),
+        pltpu.SemaphoreType.DMA((1,)),
         pltpu.SemaphoreType.DMA((N_COPIES,)),
     ]
     in_vmem = pl.BlockSpec(memory_space=pltpu.VMEM)
     in_smem = pl.BlockSpec(memory_space=pltpu.SMEM)
     in_hbm = pl.BlockSpec(memory_space=pl.ANY)
-    return pl.pallas_call(
+    both = pl.pallas_call(
         layer_kernel,
-        out_shape=(
-            jax.ShapeDtypeStruct((128, 512), BF),
-            jax.ShapeDtypeStruct((128, 512), BF),
-        ),
+        out_shape=jax.ShapeDtypeStruct((2, 128, 512), BF),
         in_specs=[in_vmem] * 4 + [in_smem] * 2 + [in_hbm] * 6,
-        out_specs=(in_vmem, in_vmem),
+        out_specs=in_vmem,
         scratch_shapes=scratch,
         name="layer",
         compiler_params=pltpu.CompilerParams(
@@ -512,6 +527,7 @@
         queries, fresh_keys, fresh_values, parents, context_len, tree_size, cached_keys, cached_values,
         gate_up_weight, down_weight, out_weight, residual,
     )
+    return both[0], both[1]
 
 
 def solution(mesh):

time: 162 us -> 145 us (0.90)
  Pallas kernels: 156 us -> 141 us
    pallas_call x1, Pallas kernels: 156 us -> 141 us  [layer(): pl.pallas_call(layer_kernel, out_shape=jax.ShapeDtypeStruct((2, 128, 512)...]
    unnamed x2 -> x0, local copies, waits for them, and re-layouts: 3.14 us -> none
    squeeze x0 -> x1, local copies, waits for them, and re-layouts: none -> 1.68 us  [layer(): return (both[0], both[1])]
where the time goes in v3:
time: 145 us
  Pallas kernels  141 us (97%)
  between operations  1.93 us (1%)
  local copies, waits for them, and re-layouts  1.68 us (1%)
    pallas_call x1, Pallas kernels, layer(): pl.pallas_call(layer_kernel, out_shape=jax.ShapeDtypeStruct((2, 128, 512)...  141 us

profile of v3, /device:TPU:8, one launch (start us, length us, event | category | flops | bytes accessed | tf_op | source)
XLA Modules:
  0.0 144.7 jit_solution(18173127778922960831)
XLA Ops:
  1.9 141.0 %layer.1 = bf16[2,128,512]{2,1,0:T(8,128)(2,1)} custom-call(bf16[64,1024]{1,0:T(8,128)(2,1)} %queries.1, bf16[64,128]{1,0:T(8,128)(2,1)} %fresh_k.1, bf16[64,128]{1,0:T(8,128)(2,1)} %fresh_v.1, s32[1,64]{1,0:T(1,128)} %parents.1, s32[1]{0:T(128)S(6)} %copy.14.length, s32[1]{0:T(128)S(6)} %copy.15.live, bf16[1,2048,128]{2,1,0:T(8,128)(2,1)} %keys_hbm.1, ...), custom_call_target="tpu_custom_call" | custom-call | tf_op jit(solution)/shard_map/layer/pallas_call | solution.py:516
  143.0 1.7 %slice_bitcast_fusion = (bf16[128,512]{1,0:T(8,128)(2,1)}, bf16[128,512]{1,0:T(8,128)(2,1)}) fusion(bf16[2,128,512]{2,1,0:T(8,128)(2,1)} %layer.1), kind=kLoop, calls=%fused_computation | loop fusion | bytes 524288 | tf_op jit(solution)/shard_map/squeeze | solution.py:530

commit v4 on v3

v4 whole, which is shorter than its diff:
```python
import math

import jax
import jax.numpy as jnp
from jax import lax
from jax.experimental import pallas as pl
from jax.experimental.pallas import tpu as pltpu
from jax.sharding import PartitionSpec as P

D = 8192
HD = 128
CTX = 2048
TREE = 64

epsilon = 1e-05

BF = jnp.bfloat16
F32 = jnp.float32
MESH = pl.DeviceIdType.MESH

A_U = 512
B_U = 384
A_W = 2 * A_U
B_W = 2 * B_U
HALF = 2 * A_U + 2 * B_U
H_OFF = (0, A_U, 2 * A_U, 2 * A_U + B_U)
OTHERS = ((0, 1), (0, 3), (1, 0), (0, 2), (1, 1), (1, 3), (1, 2))

NR = (16, 32, 16)
ROW0 = (0, 16, 48)
TWO_HOPS = ()

ORDER = (
    0, 17, 81, 1, 145, 21, 19, 18, 24, 2, 23, 22, 20, 3, 84, 4, 85, 83, 87, 86, 82, 25, 88, 5, 6,
    89, 149, 148, 7, 146, 151, 8, 152, 9, 26, 10, 11, 150, 12, 90, 13, 147, 30, 14, 29, 33, 32, 31,
    27, 28, 15, 153, 34, 91, 16, 93, 56, 95, 92, 55, 96, 97, 94, 37, 154, 98, 101, 57, 120, 39, 58,
    155, 119, 161, 160, 157, 156, 158, 38, 159, 102, 122, 61, 162, 103, 42, 35, 121, 99, 166, 106,
    183, 165, 124, 40, 104, 100, 125, 168, 60, 109, 185, 167, 64, 127, 43, 107, 45, 128, 63, 113,
    171, 36, 163, 184, 188, 49, 110, 46, 131, 130, 186, 118, 112, 191, 67, 170, 66, 164, 48, 123,
    132, 136, 105, 189, 114, 115, 174, 137, 54, 173, 126, 108, 133, 192, 195, 72, 134, 73, 117, 177,
    116, 138, 176, 194, 129, 111, 41, 59, 74, 135, 139, 68, 182, 51, 187, 200, 69, 196, 50, 62, 201,
    44, 140, 169, 178, 179, 141, 197, 190, 71, 172, 52, 70, 53, 47, 198, 180, 75, 65, 181, 142, 199,
    175, 193, 203, 76, 202, 77, 204, 205, 78, 143, 206, 79, 207, 144, 80, 208,
)


def layer_kernel(
    queries, fresh_k, fresh_v, parents, length, live, keys_hbm, values_hbm,
    gw, dw, wo_hbm, res_hbm,
    out,
    KS, VS, FK, FV, S, PR, TB, ATT,
    G, R0, R1, WC, DD, WO, RES, PP, RB, X, PA, PB, RA, RAX, RBX, RBY, SQ, SQR, SC, H, PDO, PDS, PDI, FR, FS, FXR, OS, OXR,
    lsem, ssem, rsem,
):
    h = lax.axis_index("head")
    w = lax.axis_index("wide")
    xh = w // 8
    y = (w // 2) % 4
    c = w % 2
    flip = 1 - 2 * c
    xo = 1 - xh

    def wide(dxh, dy):
        return (((xh + dxh + 2) % 2) * 4 + (y + dy + 4) % 4) * 2 + c

    sib = (h, w + flip)
    xl = h // 4
    z = h % 4

    def place(j):
        return 2 * (j % 4) + j // 4

    def wdev(dxh, dy):
        return (h, wide(dxh, dy))

    def hdev(k):
        return ((h + k) % 8, w)

    def zdev(n):
        return (xl * 4 + (z + n) % 4, w)

    names = {}
    sent = []

    def copy_of(i, src, dst, dev):
        return pltpu.make_async_remote_copy(
            src_ref=src, dst_ref=dst, send_sem=ssem.at[0], recv_sem=rsem.at[i],
            device_id=dev, device_id_type=MESH,
        )

    def send(name, src, dst, dev):
        i = names.setdefault(name, len(names))
        cp = copy_of(i, src, dst, dev)
        cp.start()
        sent.append(cp)

    def arrive(name, dst, dev):
        copy_of(names[name], dst, dst, dev).wait_recv()

    mine = pl.ds(pl.multiple_of(c * HALF, 128), HALF)
    other = pl.ds(pl.multiple_of((1 - c) * HALF, 128), HALF)
    loads = [
        pltpu.make_async_copy(keys_hbm.at[0], KS, lsem.at[0]),
        pltpu.make_async_copy(values_hbm.at[0], VS, lsem.at[1]),
        pltpu.make_async_copy(gw.at[:, :, mine], R0, lsem.at[2]),
        pltpu.make_async_copy(wo_hbm, WO, lsem.at[3]),
        pltpu.make_async_copy(
            res_hbm.at[pl.ds(pl.multiple_of(h * 128, 128), 128), :], RES, lsem.at[4]
        ),
        pltpu.make_async_copy(dw.at[mine, :], DD.at[0], lsem.at[5]),
    ]
    for cp in loads:
        cp.start()

    partners = [sib]
    partners += [wdev(dx, dy) for dx, dy in OTHERS]
    partners += [hdev(k) for k in range(1, 8)]
    barrier = pltpu.get_barrier_semaphore()
    for dev in partners:
        pl.semaphore_signal(barrier, inc=1, device_id=dev, device_id_type=MESH)

    def enter():
        pl.semaphore_wait(barrier, len(partners))
        send("s_gw", gw.at[:, :, other], R1, sib)

    node = lax.broadcasted_iota(jnp.int32, (TREE, TREE), 0)
    child = lax.broadcasted_iota(jnp.int32, (TREE, TREE), 1)
    linked = (parents[...] == node) | (node == child)
    reached = jnp.where(linked, 1.0, 0.0).astype(BF)
    for squaring in range(6):
        reached = jnp.minimum(jnp.dot(reached, reached, preferred_element_type=F32), 1.0).astype(BF)
    same = jnp.where(node == child, 1.0, 0.0).astype(BF)
    visible = lax.dot_general(reached, same, (((0,), (0,)), ((), ())), preferred_element_type=F32)
    TB[...] = jnp.full((TREE, 128), -1e30, F32)
    TB[:, 0:TREE] = jnp.where((visible > 0.5) & (child < live[0]), 0.0, -1e30)
    FK[0:TREE] = fresh_k[...]
    FK[TREE:128] = jnp.zeros((128 - TREE, HD), BF)
    FV[0:TREE] = fresh_v[...]
    FV[TREE:128] = jnp.zeros((128 - TREE, HD), BF)
    positions = lax.broadcasted_iota(jnp.int32, (1, CTX), 1)
    cache_bias = jnp.where(positions < length[0], 0.0, -1e30)
    score_scale = math.log2(math.e) / math.sqrt(HD)

    def attend(t):
        if t == 0:
            loads[0].wait()
        r0, nr = ROW0[t], NR[t]
        m8 = 8 * nr
        q = jnp.concatenate([queries[r0 : r0 + nr, j * HD : (j + 1) * HD] for j in range(8)], axis=0)
        trans = (((1,), (1,)), ((), ()))

        @pl.loop(0, CTX // 512)
        def _(i):
            n = pl.ds(pl.multiple_of(i * 512, 512), 512)
            S[0:m8, n] = lax.dot_general(q, KS[n, :], trans, preferred_element_type=F32)

        S[0:m8, CTX : CTX + 128] = lax.dot_general(q, FK[...], trans, preferred_element_type=F32)
        if t == 0:
            loads[1].wait()
        alive = lax.broadcasted_iota(jnp.int32, (nr, 1), 0) + r0 < live[0]
        denominators = []
        strips = nr // 16
        for j in range(8 * strips):
            r = slice(16 * j, 16 * j + 16)
            n0 = r0 + 16 * (j % strips)
            cache = S[r, 0:CTX] + cache_bias
            tree = S[r, CTX : CTX + 128] + TB[n0 : n0 + 16, :]
            row_max = jnp.maximum(
                jnp.max(cache, axis=1, keepdims=True), jnp.max(tree, axis=1, keepdims=True)
            )
            cache = jnp.exp2((cache - row_max) * score_scale)
            tree = jnp.exp2((tree - row_max) * score_scale)
            denominators.append(
                jnp.sum(cache, axis=1, keepdims=True) + jnp.sum(tree, axis=1, keepdims=True)
            )
            PR[r, 0:CTX] = cache.astype(BF)
            PR[r, CTX : CTX + 128] = tree.astype(BF)
        mixed = jnp.dot(PR[0:m8, 0:CTX], VS[...], preferred_element_type=F32)
        mixed = mixed + jnp.dot(PR[0:m8, CTX : CTX + 128], FV[...], preferred_element_type=F32)
        for j in range(8):
            below = jnp.concatenate(denominators[strips * j : strips * j + strips], axis=0)
            part = mixed[nr * j : nr * j + nr] / below
            ATT[t][:, j * HD : (j + 1) * HD] = jnp.where(alive, part, 0.0).astype(BF)
        for dx, dy in OTHERS:
            send(f"g{t}{dx}{dy}", ATT[t], G[t].at[w], wdev(dx, dy))
        send(f"gc{t}", ATT[t], G[t].at[w], sib)
        G[t][w] = ATT[t][...]

    def gather_on(t, dx, dy):
        src = wide(-dx, -dy)
        arrive(f"g{t}{dx}{dy}", G[t].at[src], wdev(-dx, -dy))
        send(f"gc{t}", G[t].at[src], G[t].at[src], sib)

    def untwist(k):
        if k == 0:
            loads[2].wait()
        if k == 8:
            arrive("s_gw", R1, sib)
        raw = R0 if k < 8 else R1
        i = k % 8
        b = raw[64 * i : 64 * i + 64]
        gate, up = b[:, 0, :], b[:, 1, :]
        o = slice(64 * k, 64 * k + 64)
        for p in range(4):
            n = A_U if p < 2 else B_U
            u = H_OFF[p]
            WC[o, 2 * u : 2 * u + n] = gate[:, u : u + n]
            WC[o, 2 * u + n : 2 * u + 2 * n] = up[:, u : u + n]

    def project(t):
        arrive(f"gc{t}", G[t].at[0:8], sib)
        if t == 0:
            loads[3].wait()
        L = 2 * NR[t]
        rows = G[t][...].reshape(8 * L, 1024)
        part = jnp.dot(rows, WO[...], preferred_element_type=F32).astype(BF).reshape(8, L, 512)
        for j in range(8):
            PP[t][place(j)] = part[j]
        if t == len(NR) - 1:
            send("s_dw", dw.at[other, :], DD.at[1], sib)
        if t in TWO_HOPS:
            for n in (1, 3, 2):
                pair = pl.ds(2 * ((z + n) % 4), 2)
                send(f"o{t}", PP[t].at[pair], RB[t].at[2 * n - 2 : 2 * n], zdev(n))
            return
        for k in range(1, 8):
            send(f"o{t}", PP[t].at[place((h + k) % 8)], RB[t].at[k - 1], hdev(k))

    def z_sum(t, e):
        total = PP[t][2 * z + e].astype(F32)
        for n in range(3):
            total = total + RB[t][2 * n + e].astype(F32)
        return total

    def other_half(t):
        arrive(f"o{t}", RB[t].at[0:6], hdev(1))
        OS[t][...] = z_sum(t, 1 - xl).astype(BF)
        send(f"ox{t}", OS[t], OXR[t], hdev(4))

    def combine(t):
        if t == 0:
            loads[4].wait()
        r0, nr = ROW0[t], NR[t]
        rows = (slice(r0, r0 + nr), slice(64 + r0, 64 + r0 + nr))
        total = jnp.concatenate([RES[r, :] for r in rows], axis=0).astype(F32)
        if t in TWO_HOPS:
            total = total + z_sum(t, xl)
            arrive(f"ox{t}", OXR[t], hdev(4))
            total = total + OXR[t][...].astype(F32)
        else:
            total = total + PP[t][place(h)].astype(F32)
            arrive(f"o{t}", RB[t], hdev(1))
            for k in range(7):
                total = total + RB[t][k].astype(F32)
        rounded = total.astype(BF)
        own = X[t].at[place(h), :, 0:512]
        own[...] = rounded
        if t in TWO_HOPS:
            send(f"xx_{t}", own, own, hdev(4))
        else:
            for k in range(1, 8):
                send(f"x{t}{k}", own, own, hdev(k))
        send(f"xc{t}", own, X[t].at[place(h), :, 512:1024], sib)
        out[0, rows[0], :] = rounded[0:nr]
        out[0, rows[1], :] = rounded[nr : 2 * nr]

    def spread_pair(t):
        one = 2 * z + 1 - xl
        arrive(f"xx_{t}", X[t].at[one, :, 0:512], hdev(4))
        both = X[t].at[pl.ds(2 * z, 2), :, 0:512]
        for n in (1, 3, 2):
            send(f"x{t}{n}", both, both, zdev(n))
        send(f"xc{t}", X[t].at[one, :, 0:512], X[t].at[one, :, 512:1024], sib)

    def spread(t, k):
        if t in TWO_HOPS:
            j = pl.ds(2 * ((z + 4 - k) % 4), 2)
            arrive(f"x{t}{k}", X[t].at[j, :, 0:512], zdev(4 - k))
        else:
            j = place((h + 8 - k) % 8)
            arrive(f"x{t}{k}", X[t].at[j, :, 0:512], hdev(8 - k))
        send(f"xc{t}", X[t].at[j, :, 0:512], X[t].at[j, :, 512:1024], sib)

    def spread_end(t):
        arrive(f"xc{t}", X[t].at[:, :, 512:1024], sib)

    step_dev = [wdev(0, 1), wdev(0, 3)]
    from_dev = [wdev(0, 3), wdev(0, 1)]
    xdev = wdev(1, 0)

    def first(d, s):
        return (y + 3 - s + 4) % 4 if d == 0 else (y + 1 + s) % 4

    def product(t, out, col0, width):
        @pl.loop(0, width // 256)
        def _(i):
            rows = X[t][...].reshape(16 * NR[t], 1024)
            cols = pl.ds(pl.multiple_of(col0 + i * 256, 256), 256)
            part = jnp.dot(rows, WC[:, cols], preferred_element_type=F32).astype(BF)
            out[:, :, :, pl.ds(pl.multiple_of(i * 256, 256), 256)] = part.reshape(4, 2, 2 * NR[t], 256)

    def a_piece(t, d):
        product(t, PA[t].at[d], d * A_W, A_W)
        send(f"a{t}{d}0", PA[t].at[d, first(d, 0)], RA[t].at[d, 0], step_dev[d])

    def b_piece(t, d):
        product(t, PB[t].at[d], 2 * A_W + d * B_W, B_W)
        for s in range(4):
            g = first(d, s)
            send(f"bx{t}{d}{s}", PB[t].at[d, g, xo], RBX[t].at[d, s], xdev)

    def squares(t):
        ones = jnp.ones((8, 1024), BF)
        for b in range(8):
            v = X[t][b].astype(F32)
            part = lax.dot_general(
                ones, (v * v).astype(BF), (((1,), (1,)), ((), ())), preferred_element_type=F32
            )
            SQ[t][b] = jnp.concatenate([part] * (64 // NR[t]), axis=1)
        for n, (dx, dy) in enumerate(OTHERS):
            b = ((y + dy) % 4) * 2 + (xh + dx) % 2
            send(f"q{t}", SQ[t].at[b], SQR[t].at[n], wdev(dx, dy))

    def row_scale(t):
        total = SQ[t][y * 2 + xh]
        arrive(f"q{t}", SQR[t], wdev(0, 1))
        for n in range(7):
            total = total + SQR[t][n]
        scale = lax.rsqrt(jnp.transpose(total)[0 : 2 * NR[t], 0:1] / D + epsilon)
        SC[t][...] = jnp.broadcast_to(scale, (2 * NR[t], 128))

    def add(out, left, right):
        for i in range(out.shape[0] // 32):
            r = slice(32 * i, 32 * i + 32)
            out[r, :] = (left[r, :].astype(F32) + right[r, :].astype(F32)).astype(BF)

    def a_step(t, d, s):
        g = first(d, s)
        arrive(f"a{t}{d}{s - 1}", RA[t].at[d, s - 1], from_dev[d])
        for e in range(2):
            add(PA[t].at[d, g, e], PA[t].at[d, g, e], RA[t].at[d, s - 1, e])
        if s < 3:
            send(f"a{t}{d}{s}", PA[t].at[d, g], RA[t].at[d, s], step_dev[d])
        else:
            send(f"xx{t}{d}", PA[t].at[d, y, xo], RAX[t].at[d], xdev)

    def b_sum(t, d, s):
        g = first(d, s)
        out = PB[t].at[d, g, xh]
        arrive(f"bx{t}{d}{s}", RBX[t].at[d, s], xdev)
        add(out, out, RBX[t].at[d, s])
        if s and s < 3:
            arrive(f"b{t}{d}{s - 1}", RBY[t].at[d, s - 1], from_dev[d])
            add(out, out, RBY[t].at[d, s - 1])
        if s < 3:
            send(f"b{t}{d}{s}", out, RBY[t].at[d, s], step_dev[d])

    def gated(t, left, right, n, col0):
        scale = SC[t][:, 0:1]
        gate = (left[:, 0:n].astype(F32) + right[:, 0:n].astype(F32)) * scale
        up = (left[:, n : 2 * n].astype(F32) + right[:, n : 2 * n].astype(F32)) * scale
        H[t][y, xh, :, col0 : col0 + n] = (gate / (1.0 + jnp.exp(-gate)) * up).astype(BF)

    def cols(part, d):
        o = H_OFF[2 * part + d]
        return slice(o, o + (A_U, B_U)[part])

    def b_end(t, d):
        b_sum(t, d, 3)
        arrive(f"b{t}{d}2", RBY[t].at[d, 2], from_dev[d])
        gated(t, PB[t].at[d, y, xh], RBY[t].at[d, 2], B_U, H_OFF[2 + d])
        piece = H[t].at[y, xh, :, cols(1, d)]
        send(f"hb{t}{d}0", piece, piece, step_dev[d])
        send(f"hx{t}{d}9", piece, piece, xdev)

    def hb_step(t, d, s):
        piece = H[t].at[first(d, s), xh, :, cols(1, d)]
        arrive(f"hb{t}{d}{s}", piece, from_dev[d])
        if s < 2:
            send(f"hb{t}{d}{s + 1}", piece, piece, step_dev[d])
        send(f"hx{t}{d}{s}", piece, piece, xdev)

    def a_end(t, d):
        arrive(f"xx{t}{d}", RAX[t].at[d], xdev)
        gated(t, PA[t].at[d, y, xh], RAX[t].at[d], A_U, H_OFF[d])
        piece = H[t].at[y, xh, :, cols(0, d)]
        send(f"ho{t}{d}0", piece, piece, step_dev[d])
        send(f"hp{t}{d}9", piece, piece, xdev)

    def ha_step(t, d, s, q):
        if s == 9:
            piece = H[t].at[y, xo, :, cols(0, d)]
            arrive(f"hp{t}{d}9", piece, xdev)
            send(f"hp{t}{d}0", piece, piece, step_dev[d])
            return
        piece = H[t].at[first(d, s), xh if q == "o" else xo, :, cols(0, d)]
        arrive(f"h{q}{t}{d}{s}", piece, from_dev[d])
        if s < 2:
            send(f"h{q}{t}{d}{s + 1}", piece, piece, step_dev[d])

    down_ready = []

    def down(t, i):
        if not down_ready:
            loads[5].wait()
            arrive("s_dw", DD.at[1], sib)
            down_ready.append(True)
        steps = ((9,), (1,), (0, 2))[i]
        for s in steps:
            for d in range(2):
                g = y if s == 9 else first(d, s)
                arrive(f"hx{t}{d}{s}", H[t].at[g, xo, :, cols(1, d)], xdev)
                if s == 2:
                    ha_step(t, d, 2, "o")
                    ha_step(t, d, 2, "p")
        gs = ((y,), ((y + 2) % 4,), ((y + 1) % 4, (y + 3) % 4))[i]
        for e, out in ((1, PDS), (0, PDO)):
            @pl.loop(0, 2)
            def _(n):
                n = pl.ds(pl.multiple_of(n * 256, 256), 256)
                rows = jnp.concatenate([H[t][g].reshape(4 * NR[t], HALF) for g in gs], axis=0)
                part = jnp.dot(rows, DD[e, :, n], preferred_element_type=F32).astype(BF)
                for m, g in enumerate(gs):
                    block = part[4 * NR[t] * m : 4 * NR[t] * (m + 1)].reshape(2, 2 * NR[t], 256)
                    out[t][pl.ds(2 * g, 2), :, n] = block

            if e:
                for m, g in enumerate(gs):
                    pair = pl.ds(2 * g, 2)
                    send(f"sh{t}{i}{m}", PDS[t].at[pair], PDI[t].at[pair], sib)

    def share(t, i):
        gs = ((y,), ((y + 2) % 4,), ((y + 1) % 4, (y + 3) % 4))[i]
        index = names.setdefault(f"f{t}", len(names))
        for m, g in enumerate(gs):
            pair = pl.ds(2 * g, 2)
            arrive(f"sh{t}{i}{m}", PDI[t].at[pair], sib)
            for e in range(2):
                j = 2 * g + e
                add(PDO[t].at[j], PDO[t].at[j], PDI[t].at[j])

            @pl.when(g != z)
            def _():
                slot = (g - z + 4) % 4 - 1
                copy_of(index, PDO[t].at[pair], FR[t].at[slot], (xl * 4 + g, w)).start()

    def head_sum(t, e):
        total = PDO[t][2 * z + e].astype(F32)
        for n in range(3):
            total = total + FR[t][n, e].astype(F32)
        return total

    def across(t):
        arrive(f"f{t}", FR[t], hdev(1))
        for n in range(1, 4):
            g = (z + n) % 4
            sent.append(
                copy_of(names[f"f{t}"], PDO[t].at[pl.ds(2 * g, 2)], FR[t].at[n - 1], (xl * 4 + g, w))
            )
        FS[t][...] = head_sum(t, 1 - xl).astype(BF)
        send(f"fx{t}", FS[t], FXR[t], hdev(4))

    def finish(t):
        total = head_sum(t, xl)
        arrive(f"fx{t}", FXR[t], hdev(4))
        total = total + FXR[t][...].astype(F32)
        rounded = total.astype(BF)
        r0, nr = ROW0[t], NR[t]
        out[1, r0 : r0 + nr, :] = rounded[0:nr]
        out[1, 64 + r0 : 64 + r0 + nr, :] = rounded[nr : 2 * nr]

    steps = {"in": (enter,)}
    for k in range(16):
        steps[f"u{k}"] = (untwist, k)
    for t in range(len(NR)):
        steps[f"at{t}"] = (attend, t)
        for dx, dy in OTHERS:
            steps[f"gf{t}{dx}{dy}"] = (gather_on, t, dx, dy)
        steps[f"op{t}"] = (project, t)
        steps[f"cm{t}"] = (combine, t)
        if t in TWO_HOPS:
            steps[f"or{t}"] = (other_half, t)
            steps[f"xp{t}"] = (spread_pair, t)
        for k in range(1, 4 if t in TWO_HOPS else 8):
            steps[f"xf{t}{k}"] = (spread, t, k)
        steps[f"xr{t}"] = (spread_end, t)
        steps[f"sq{t}"] = (squares, t)
        steps[f"sc{t}"] = (row_scale, t)
        for d in range(2):
            steps[f"ga{t}{d}"] = (a_piece, t, d)
            steps[f"gb{t}{d}"] = (b_piece, t, d)
            for s in range(3):
                steps[f"as{t}{d}{s + 1}"] = (a_step, t, d, s + 1)
                steps[f"bs{t}{d}{s}"] = (b_sum, t, d, s)
                steps[f"hb{t}{d}{s}"] = (hb_step, t, d, s)
            steps[f"bf{t}{d}"] = (b_end, t, d)
            steps[f"af{t}{d}"] = (a_end, t, d)
            for s in (0, 1):
                for q in "op":
                    steps[f"h{q}{t}{d}{s}"] = (ha_step, t, d, s, q)
            steps[f"hp{t}{d}9"] = (ha_step, t, d, 9, "p")
        for i in range(3):
            steps[f"dn{t}{i}"] = (down, t, i)
            steps[f"fz{t}{i}"] = (share, t, i)
        steps[f"fx{t}"] = (across, t)
        steps[f"fo{t}"] = (finish, t)
    table = list(steps.values())
    assert sorted(ORDER) == list(range(len(table)))
    for number in ORDER:
        step, *where = table[number]
        step(*where)

    assert len(names) <= N_COPIES
    for cp in sent:
        cp.wait_send()


N_COPIES = 224


def layer(
    queries, fresh_keys, fresh_values, cached_keys, cached_values, context_len, tree_size, parents,
    residual, out_weight, gate_up_weight, down_weight,
):
    vm = pltpu.VMEM

    def parts(per_row, *shape):
        return tuple(vm(tuple(x or per_row * n for x in shape), BF) for n in NR)

    scratch = [
        vm((CTX, HD), BF),
        vm((CTX, HD), BF),
        vm((128, HD), BF),
        vm((128, HD), BF),
        vm((256, CTX + 128), F32),
        vm((256, CTX + 128), BF),
        vm((TREE, 128), F32),
        parts(1, 0, 1024),
        parts(1, 16, 0, 1024),
        vm((512, 2, HALF), BF),
        vm((512, 2, HALF), BF),
        vm((1024, 2 * HALF), BF),
        vm((2, HALF, 512), BF),
        vm((1024, 512), BF),
        vm((128, 512), BF),
        parts(2, 8, 0, 512),
        parts(2, 7, 0, 512),
        parts(2, 8, 0, 1024),
        parts(2, 2, 4, 2, 0, A_W),
        parts(2, 2, 4, 2, 0, B_W),
        parts(2, 2, 3, 2, 0, A_W),
        parts(2, 2, 0, A_W),
        parts(2, 2, 4, 0, B_W),
        parts(2, 2, 3, 0, B_W),
        tuple(vm((8, 8, 128), F32) for n in NR),
        tuple(vm((7, 8, 128), F32) for n in NR),
        tuple(vm((2 * n, 128), F32) for n in NR),
        parts(2, 4, 2, 0, HALF),
        parts(2, 8, 0, 512),
        parts(2, 8, 0, 512),
        parts(2, 8, 0, 512),
        parts(2, 3, 2, 0, 512),
        parts(2, 0, 512),
        parts(2, 0, 512),
        parts(2, 0, 512),
        parts(2, 0, 512),
        pltpu.SemaphoreType.DMA((6,)),
        pltpu.SemaphoreType.DMA((1,)),
        pltpu.SemaphoreType.DMA((N_COPIES,)),
    ]
    in_vmem = pl.BlockSpec(memory_space=pltpu.VMEM)
    in_smem = pl.BlockSpec(memory_space=pltpu.SMEM)
    in_hbm = pl.BlockSpec(memory_space=pl.ANY)
    both = pl.pallas_call(
        layer_kernel,
        out_shape=jax.ShapeDtypeStruct((2, 128, 512), BF),
        in_specs=[in_vmem] * 4 + [in_smem] * 2 + [in_hbm] * 6,
        out_specs=in_vmem,
        scratch_shapes=scratch,
        name="layer",
        compiler_params=pltpu.CompilerParams(
            collective_id=0, has_side_effects=True, vmem_limit_bytes=60 << 20
        ),
    )(
        queries, fresh_keys, fresh_values, parents, context_len, tree_size, cached_keys, cached_values,
        gate_up_weight, down_weight, out_weight, residual,
    )
    return both[0], both[1]


def solution(mesh):
    placed = (
        P("wide", "head"),
        P("wide", "head"),
        P("wide", "head"),
        P("wide", None, "head"),
        P("wide", None, "head"),
        P("wide"),
        P("wide"),
        P("wide", None),
        P(None, "wide"),
        P("head", "wide"),
        P("wide", None, "head"),
        P("head", "wide"),
    )
    return jax.shard_map(
        layer,
        mesh=mesh,
        in_specs=placed,
        out_specs=(P("head", "wide"), P("head", "wide")),
        check_vma=False,
    )
```

time: 145 us -> 140 us (0.966)
  Pallas kernels: 141 us -> 136 us
    pallas_call x1, Pallas kernels: 141 us -> 136 us  [layer(): pl.pallas_call(layer_kernel, out_shape=jax.ShapeDtypeStruct((2, 128, 512)...]
where the time goes in v4:
time: 140 us
  Pallas kernels  136 us (97%)
  between operations  1.93 us (1%)
  local copies, waits for them, and re-layouts  1.68 us (1%)
    pallas_call x1, Pallas kernels, layer(): pl.pallas_call(layer_kernel, out_shape=jax.ShapeDtypeStruct((2, 128, 512)...  136 us

profile of v4, /device:TPU:8, one launch (start us, length us, event | category | flops | bytes accessed | tf_op | source)
XLA Modules:
  0.0 140.1 jit_solution(15033252584760591890)
XLA Ops:
  1.9 136.5 %layer.1 = bf16[2,128,512]{2,1,0:T(8,128)(2,1)} custom-call(bf16[64,1024]{1,0:T(8,128)(2,1)} %queries.1, bf16[64,128]{1,0:T(8,128)(2,1)} %fresh_k.1, bf16[64,128]{1,0:T(8,128)(2,1)} %fresh_v.1, s32[1,64]{1,0:T(1,128)} %parents.1, s32[1]{0:T(128)S(6)} %copy.14.length, s32[1]{0:T(128)S(6)} %copy.15.live, bf16[1,2048,128]{2,1,0:T(8,128)(2,1)} %keys_hbm.1, ...), custom_call_target="tpu_custom_call" | custom-call | tf_op jit(solution)/shard_map/layer/pallas_call | solution.py:574
  138.4 1.7 %slice_bitcast_fusion = (bf16[128,512]{1,0:T(8,128)(2,1)}, bf16[128,512]{1,0:T(8,128)(2,1)}) fusion(bf16[2,128,512]{2,1,0:T(8,128)(2,1)} %layer.1), kind=kLoop, calls=%fused_computation | loop fusion | bytes 524288 | tf_op jit(solution)/shard_map/squeeze | solution.py:588

commit v5 on v4

--- a/solution.py
+++ b/solution.py
@@ -28,19 +28,20 @@
 
 NR = (16, 32, 16)
 ROW0 = (0, 16, 48)
+LAST = len(NR) - 1
 TWO_HOPS = ()
 
 ORDER = (
-    0, 17, 81, 1, 145, 21, 19, 18, 24, 2, 23, 22, 20, 3, 84, 4, 85, 83, 87, 86, 82, 25, 88, 5, 6,
-    89, 149, 148, 7, 146, 151, 8, 152, 9, 26, 10, 11, 150, 12, 90, 13, 147, 30, 14, 29, 33, 32, 31,
-    27, 28, 15, 153, 34, 91, 16, 93, 56, 95, 92, 55, 96, 97, 94, 37, 154, 98, 101, 57, 120, 39, 58,
-    155, 119, 161, 160, 157, 156, 158, 38, 159, 102, 122, 61, 162, 103, 42, 35, 121, 99, 166, 106,
-    183, 165, 124, 40, 104, 100, 125, 168, 60, 109, 185, 167, 64, 127, 43, 107, 45, 128, 63, 113,
-    171, 36, 163, 184, 188, 49, 110, 46, 131, 130, 186, 118, 112, 191, 67, 170, 66, 164, 48, 123,
-    132, 136, 105, 189, 114, 115, 174, 137, 54, 173, 126, 108, 133, 192, 195, 72, 134, 73, 117, 177,
-    116, 138, 176, 194, 129, 111, 41, 59, 74, 135, 139, 68, 182, 51, 187, 200, 69, 196, 50, 62, 201,
-    44, 140, 169, 178, 179, 141, 197, 190, 71, 172, 52, 70, 53, 47, 198, 180, 75, 65, 181, 142, 199,
-    175, 193, 203, 76, 202, 77, 204, 205, 78, 143, 206, 79, 207, 144, 80, 208,
+    0, 17, 81, 145, 22, 20, 1, 2, 19, 23, 21, 82, 18, 24, 3, 4, 25, 85, 83, 86, 88, 84, 87, 5, 6,
+    150, 89, 152, 147, 151, 7, 148, 146, 149, 8, 26, 153, 9, 10, 11, 90, 12, 27, 13, 32, 28, 30, 29,
+    31, 14, 33, 15, 16, 34, 37, 56, 92, 55, 95, 91, 93, 94, 96, 97, 38, 39, 58, 98, 101, 57, 154,
+    61, 119, 42, 120, 64, 40, 157, 99, 158, 103, 122, 161, 155, 160, 121, 156, 159, 102, 162, 165,
+    184, 183, 106, 166, 167, 60, 124, 100, 35, 43, 104, 163, 186, 170, 109, 168, 125, 185, 127, 107,
+    46, 128, 63, 113, 188, 189, 36, 173, 45, 110, 130, 67, 114, 131, 164, 171, 191, 112, 177, 192,
+    123, 118, 48, 132, 49, 105, 66, 136, 174, 195, 194, 115, 126, 137, 108, 133, 41, 182, 176, 116,
+    50, 134, 54, 111, 129, 59, 72, 187, 44, 68, 200, 73, 135, 169, 62, 117, 139, 138, 69, 52, 178,
+    196, 190, 47, 51, 197, 172, 70, 179, 140, 141, 53, 71, 198, 180, 65, 193, 75, 199, 181, 175,
+    142, 77, 201, 76, 78, 74, 143, 202, 79, 144, 203, 80,
 )
 
 
@@ -429,6 +430,33 @@
                     pair = pl.ds(2 * g, 2)
                     send(f"sh{t}{i}{m}", PDS[t].at[pair], PDI[t].at[pair], sib)
 
+    def down_whole(t):
+        for s in (9, 1, 0, 2):
+            for d in range(2):
+                g = y if s == 9 else first(d, s)
+                arrive(f"hx{t}{d}{s}", H[t].at[g, xo, :, cols(1, d)], xdev)
+                if s == 2:
+                    ha_step(t, d, 2, "o")
+                    ha_step(t, d, 2, "p")
+        for e, to in ((1, PDS), (0, PDO)):
+            @pl.loop(0, 2)
+            def _(n):
+                n = pl.ds(pl.multiple_of(n * 256, 256), 256)
+                rows = H[t][...].reshape(16 * NR[t], HALF)
+                part = jnp.dot(rows, DD[e, :, n], preferred_element_type=F32).astype(BF)
+                to[t][:, :, n] = part.reshape(8, 2 * NR[t], 256)
+
+            if e:
+                send(f"sh{t}", PDS[t], PDI[t], sib)
+
+    def share_whole(t):
+        arrive(f"sh{t}", PDI[t], sib)
+        for k in range(1, 9):
+            j = place((h + k) % 8)
+            add(PDO[t].at[j], PDO[t].at[j], PDI[t].at[j])
+            if k < 8:
+                send(f"f{t}", PDO[t].at[j], FR[t].at[k - 1], hdev(k))
+
     def share(t, i):
         gs = ((y,), ((y + 2) % 4,), ((y + 1) % 4, (y + 3) % 4))[i]
         index = names.setdefault(f"f{t}", len(names))
@@ -442,28 +470,34 @@
             @pl.when(g != z)
             def _():
                 slot = (g - z + 4) % 4 - 1
-                copy_of(index, PDO[t].at[pair], FR[t].at[slot], (xl * 4 + g, w)).start()
+                copy_of(index, PDO[t].at[pair], FR[t].at[pl.ds(2 * slot, 2)], (xl * 4 + g, w)).start()
 
     def head_sum(t, e):
         total = PDO[t][2 * z + e].astype(F32)
         for n in range(3):
-            total = total + FR[t][n, e].astype(F32)
+            total = total + FR[t][2 * n + e].astype(F32)
         return total
 
     def across(t):
-        arrive(f"f{t}", FR[t], hdev(1))
+        arrive(f"f{t}", FR[t].at[0:6], hdev(1))
         for n in range(1, 4):
             g = (z + n) % 4
             sent.append(
-                copy_of(names[f"f{t}"], PDO[t].at[pl.ds(2 * g, 2)], FR[t].at[n - 1], (xl * 4 + g, w))
+                copy_of(names[f"f{t}"], PDO[t].at[pl.ds(2 * g, 2)], FR[t].at[2 * n - 2 : 2 * n], (xl * 4 + g, w))
             )
         FS[t][...] = head_sum(t, 1 - xl).astype(BF)
         send(f"fx{t}", FS[t], FXR[t], hdev(4))
 
     def finish(t):
-        total = head_sum(t, xl)
-        arrive(f"fx{t}", FXR[t], hdev(4))
-        total = total + FXR[t][...].astype(F32)
+        if t == LAST:
+            arrive(f"f{t}", FR[t], hdev(1))
+            total = PDO[t][place(h)].astype(F32)
+            for n in range(7):
+                total = total + FR[t][n].astype(F32)
+        else:
+            total = head_sum(t, xl)
+            arrive(f"fx{t}", FXR[t], hdev(4))
+            total = total + FXR[t][...].astype(F32)
         rounded = total.astype(BF)
         r0, nr = ROW0[t], NR[t]
         out[1, r0 : r0 + nr, :] = rounded[0:nr]
@@ -499,10 +533,14 @@
                 for q in "op":
                     steps[f"h{q}{t}{d}{s}"] = (ha_step, t, d, s, q)
             steps[f"hp{t}{d}9"] = (ha_step, t, d, 9, "p")
-        for i in range(3):
-            steps[f"dn{t}{i}"] = (down, t, i)
-            steps[f"fz{t}{i}"] = (share, t, i)
-        steps[f"fx{t}"] = (across, t)
+        if t == LAST:
+            steps[f"dn{t}"] = (down_whole, t)
+            steps[f"fz{t}"] = (share_whole, t)
+        else:
+            for i in range(3):
+                steps[f"dn{t}{i}"] = (down, t, i)
+                steps[f"fz{t}{i}"] = (share, t, i)
+            steps[f"fx{t}"] = (across, t)
         steps[f"fo{t}"] = (finish, t)
     table = list(steps.values())
     assert sorted(ORDER) == list(range(len(table)))
@@ -559,7 +597,7 @@
         parts(2, 8, 0, 512),
         parts(2, 8, 0, 512),
         parts(2, 8, 0, 512),
-        parts(2, 3, 2, 0, 512),
+        parts(2, 7, 0, 512),
         parts(2, 0, 512),
         parts(2, 0, 512),
         parts(2, 0, 512),

time: 140 us -> 138 us (0.986)
  Pallas kernels: 136 us -> 133 us
    pallas_call x1, Pallas kernels: 136 us -> 133 us  [layer(): pl.pallas_call(layer_kernel, out_shape=jax.ShapeDtypeStruct((2, 128, 512)...]
where the time goes in v5:
time: 138 us; the launch traced here: 137 us
  Pallas kernels  133 us (96%)
  between operations  1.93 us (1%)
  local copies, waits for them, and re-layouts  1.68 us (1%)
    pallas_call x1, Pallas kernels, layer(): pl.pallas_call(layer_kernel, out_shape=jax.ShapeDtypeStruct((2, 128, 512)...  133 us

profile of v5, /device:TPU:8, one launch (start us, length us, event | category | flops | bytes accessed | tf_op | source)
XLA Modules:
  0.0 137.1 jit_solution(946967191207770014)
XLA Ops:
  1.9 133.5 %layer.1 = bf16[2,128,512]{2,1,0:T(8,128)(2,1)} custom-call(bf16[64,1024]{1,0:T(8,128)(2,1)} %queries.1, bf16[64,128]{1,0:T(8,128)(2,1)} %fresh_k.1, bf16[64,128]{1,0:T(8,128)(2,1)} %fresh_v.1, s32[1,64]{1,0:T(1,128)} %parents.1, s32[1]{0:T(128)S(6)} %copy.14.length, s32[1]{0:T(128)S(6)} %copy.15.live, bf16[1,2048,128]{2,1,0:T(8,128)(2,1)} %keys_hbm.1, ...), custom_call_target="tpu_custom_call" | custom-call | tf_op jit(solution)/shard_map/layer/pallas_call | solution.py:612
  135.4 1.7 %slice_bitcast_fusion = (bf16[128,512]{1,0:T(8,128)(2,1)}, bf16[128,512]{1,0:T(8,128)(2,1)}) fusion(bf16[2,128,512]{2,1,0:T(8,128)(2,1)} %layer.1), kind=kLoop, calls=%fused_computation | loop fusion | bytes 524288 | tf_op jit(solution)/shard_map/squeeze | solution.py:626

commit v6 on v5

--- a/solution.py
+++ b/solution.py
@@ -372,14 +372,14 @@
         gated(t, PB[t].at[d, y, xh], RBY[t].at[d, 2], B_U, H_OFF[2 + d])
         piece = H[t].at[y, xh, :, cols(1, d)]
         send(f"hb{t}{d}0", piece, piece, step_dev[d])
-        send(f"hx{t}{d}9", piece, piece, xdev)
+        send(f"hx{t}9", piece, piece, xdev)
 
     def hb_step(t, d, s):
         piece = H[t].at[first(d, s), xh, :, cols(1, d)]
         arrive(f"hb{t}{d}{s}", piece, from_dev[d])
         if s < 2:
             send(f"hb{t}{d}{s + 1}", piece, piece, step_dev[d])
-        send(f"hx{t}{d}{s}", piece, piece, xdev)
+        send(f"hx{t}{1 if s == 1 else 2}", piece, piece, xdev)
 
     def a_end(t, d):
         arrive(f"xx{t}{d}", RAX[t].at[d], xdev)
@@ -401,16 +401,19 @@
 
     down_ready = []
 
+    def b_arrive(t, s):
+        groups = pl.ds(0, 2) if s == 2 else pl.ds(y if s == 9 else first(0, 1), 1)
+        arrive(f"hx{t}{s}", H[t].at[groups, xo, :, 2 * A_U : HALF], xdev)
+
     def down(t, i):
         if not down_ready:
             loads[5].wait()
             arrive("s_dw", DD.at[1], sib)
             down_ready.append(True)
         steps = ((9,), (1,), (0, 2))[i]
+        b_arrive(t, steps[-1])
         for s in steps:
             for d in range(2):
-                g = y if s == 9 else first(d, s)
-                arrive(f"hx{t}{d}{s}", H[t].at[g, xo, :, cols(1, d)], xdev)
                 if s == 2:
                     ha_step(t, d, 2, "o")
                     ha_step(t, d, 2, "p")
@@ -431,10 +434,9 @@
                     send(f"sh{t}{i}{m}", PDS[t].at[pair], PDI[t].at[pair], sib)
 
     def down_whole(t):
-        for s in (9, 1, 0, 2):
+        for s in (9, 1, 2):
+            b_arrive(t, s)
             for d in range(2):
-                g = y if s == 9 else first(d, s)
-                arrive(f"hx{t}{d}{s}", H[t].at[g, xo, :, cols(1, d)], xdev)
                 if s == 2:
                     ha_step(t, d, 2, "o")
                     ha_step(t, d, 2, "p")
@@ -553,7 +555,7 @@
         cp.wait_send()
 
 
-N_COPIES = 224
+N_COPIES = 205
 
 
 def layer(

time: 138 us -> 138 us (level)
  no operation moved by 1% of the time
where the time goes in v6:
time: 138 us; the launch traced here: 137 us
  Pallas kernels  133 us (96%)
  between operations  1.93 us (1%)
  local copies, waits for them, and re-layouts  1.68 us (1%)
    pallas_call x1, Pallas kernels, layer(): pl.pallas_call(layer_kernel, out_shape=jax.ShapeDtypeStruct((2, 128, 512)...  133 us

profile of v6, /device:TPU:8, one launch (start us, length us, event | category | flops | bytes accessed | tf_op | source)
XLA Modules:
  0.0 136.9 jit_solution(1219127704119064409)
XLA Ops:
  1.9 133.3 %layer.1 = bf16[2,128,512]{2,1,0:T(8,128)(2,1)} custom-call(bf16[64,1024]{1,0:T(8,128)(2,1)} %queries.1, bf16[64,128]{1,0:T(8,128)(2,1)} %fresh_k.1, bf16[64,128]{1,0:T(8,128)(2,1)} %fresh_v.1, s32[1,64]{1,0:T(1,128)} %parents.1, s32[1]{0:T(128)S(6)} %copy.14.length, s32[1]{0:T(128)S(6)} %copy.15.live, bf16[1,2048,128]{2,1,0:T(8,128)(2,1)} %keys_hbm.1, ...), custom_call_target="tpu_custom_call" | custom-call | tf_op jit(solution)/shard_map/layer/pallas_call | solution.py:614
  135.2 1.7 %slice_bitcast_fusion = (bf16[128,512]{1,0:T(8,128)(2,1)}, bf16[128,512]{1,0:T(8,128)(2,1)}) fusion(bf16[2,128,512]{2,1,0:T(8,128)(2,1)} %layer.1), kind=kLoop, calls=%fused_computation | loop fusion | bytes 524288 | tf_op jit(solution)/shard_map/squeeze | solution.py:628
